TPU v7x, 256 devices: a whole 4x4x8 slice. The times are simulated.
256 devices in a mesh: dp: 4 (over x), latent: 64 (over z, y, core).
Axes of the slice: x: 4, y: 4, z: 8, core: 2. Of those that a mesh axis runs over, the one named last changes fastest.
Arguments:
- activations: bfloat16 [1024, 4608], P('dp', 'latent'), may hold values from -6 to 6
- latent_codes: bfloat16 [1024, 256], P('dp'), may hold values from 0 to 2
- active_blocks: int32 [1024, 4], P('dp'), may hold values from 0 to 2047, all different within a row; in each aligned block of 1024 rows (0 to 1023, 1024 to 2047, ...) at most 8 rows name the same one
- decoder: bfloat16 [131072, 4608], P(('dp', 'latent')), may hold values from -0.375 to 0.375
- decoder_bias: float32 [4608], P('latent'), may hold values from -3 to 3
Outputs:
- recon_error: bfloat16 [1024, 4608], P('dp', 'latent')
- decoder_grad: bfloat16 [131072, 4608], P(('dp', 'latent'))
- codes_grad: bfloat16 [1024, 256], P('dp')
Inputs may be any that keep to these rules, and one draw needn't show every extreme that they name: `active_blocks`: each token names 4 different blocks; every block is named by at least one token and by at most 8 tokens, and some block by exactly 8.
All inputs are finite; a program needn't handle non-finite values.
Results may differ from a plain program's by a relative error of at most 0.0045.
Values may be sent and summed in bfloat16 or wider, within the bound.
A program may use at most 128 MiB of HBM per device.

v0:
```python
import jax
import jax.numpy as jnp
from jax import lax
from jax.sharding import PartitionSpec as P

LAT_BLOCK = 64
BLK_DEV = 8
K_BLK = 4


def per_device(activations, latent_codes, active_blocks, decoder, decoder_bias):
    dp_count = lax.axis_size("dp")
    lat_count = lax.axis_size("latent")
    tok_dev = activations.shape[0]
    width = decoder.shape[1]
    col_width = width // lat_count
    total_tokens = tok_dev * dp_count
    pair_count = total_tokens * K_BLK
    most = 4 * pair_count // (BLK_DEV * dp_count * lat_count)
    slot_count = BLK_DEV * most
    group = lax.axis_index("dp")
    owner = group * lat_count + lax.axis_index("latent")
    all_codes, all_blocks = (
        lax.all_gather(latent_codes, "dp", axis=0, tiled=True),
        lax.all_gather(active_blocks, "dp", axis=0, tiled=True),
    )
    flat_blocks = all_blocks.reshape(pair_count)
    local_block = flat_blocks - owner * BLK_DEV
    onehot = (local_block[:, None] == jnp.arange(BLK_DEV, dtype=jnp.int32)[None, :]).astype(
        jnp.int32
    )
    before = jnp.cumsum(onehot, axis=0) - onehot
    rank = jnp.sum(before * onehot, axis=1)
    owned = jnp.sum(onehot, axis=1) > 0
    slot_of_pair = jnp.where(owned, local_block * most + rank, -1)
    pair_index = jnp.arange(pair_count, dtype=jnp.int32)
    matched = slot_of_pair[:, None] == jnp.arange(slot_count, dtype=jnp.int32)[None, :]
    slot_pair = jnp.where(
        jnp.any(matched, axis=0),
        jnp.sum(jnp.where(matched, pair_index[:, None], 0), axis=0),
        pair_count,
    )
    flat_codes = jnp.concatenate(
        [all_codes.reshape(pair_count, LAT_BLOCK), jnp.zeros((1, LAT_BLOCK), jnp.bfloat16)], axis=0
    )
    slot_codes = flat_codes[slot_pair].reshape(BLK_DEV, most, LAT_BLOCK)
    weight_blocks = decoder.reshape(BLK_DEV, LAT_BLOCK, width)
    partial_value = jnp.einsum(
        "bsl,bld->bsd", slot_codes, weight_blocks, preferred_element_type=jnp.float32
    ).reshape(slot_count, width)
    slot_token = slot_pair // K_BLK
    dense = jax.ops.segment_sum(partial_value, slot_token, num_segments=total_tokens + 1)[
        :total_tokens
    ]
    arranged = (
        dense.reshape(dp_count, tok_dev, lat_count, col_width)
        .transpose(0, 2, 1, 3)
        .reshape(dp_count * lat_count, tok_dev, col_width)
    )
    summed = lax.psum_scatter(arranged, ("dp", "latent"), scatter_dimension=0, tiled=True)[0]
    recon_error = (summed + decoder_bias[None, :] - activations.astype(jnp.float32)).astype(
        jnp.bfloat16
    )
    whole = lax.all_gather(recon_error[None], ("dp", "latent"), axis=0, tiled=True)
    full_rows = (
        whole.reshape(dp_count, lat_count, tok_dev, col_width)
        .transpose(0, 2, 1, 3)
        .reshape(total_tokens, width)
    )
    padded_rows = jnp.concatenate([full_rows, jnp.zeros((1, width), jnp.bfloat16)], axis=0)
    slot_grad = padded_rows[slot_token]
    grad_blocks = slot_grad.reshape(BLK_DEV, most, width)
    decoder_grad = jnp.einsum(
        "bsl,bsd->bld", slot_codes, grad_blocks, preferred_element_type=jnp.float32
    )
    decoder_grad = decoder_grad.astype(jnp.bfloat16).reshape(BLK_DEV * LAT_BLOCK, width)
    slot_code_grad = jnp.einsum(
        "bsd,bld->bsl", grad_blocks, weight_blocks, preferred_element_type=jnp.float32
    )
    slot_code_grad = slot_code_grad.astype(jnp.bfloat16).reshape(slot_count, LAT_BLOCK)
    every_grad, every_pair = (
        lax.all_gather(slot_code_grad, ("dp", "latent"), axis=0, tiled=True),
        lax.all_gather(slot_pair, ("dp", "latent"), axis=0, tiled=True),
    )
    group_pairs = tok_dev * K_BLK
    mine = every_pair - group * group_pairs
    target = jnp.where((mine >= 0) & (mine < group_pairs), mine, group_pairs)
    collected = jax.ops.segment_sum(
        every_grad.astype(jnp.float32), target, num_segments=group_pairs + 1
    )[:group_pairs]
    codes_grad = collected.reshape(tok_dev, K_BLK * LAT_BLOCK).astype(jnp.bfloat16)
    return (recon_error, decoder_grad, codes_grad)


def solution(mesh):
    in_specs = (
        P("dp", "latent"),
        P("dp", None),
        P("dp", None),
        P(("dp", "latent"), None),
        P("latent"),
    )
    out_specs = (P("dp", "latent"), P(("dp", "latent"), None), P("dp", None))
    return jax.shard_map(
        per_device, mesh=mesh, in_specs=in_specs, out_specs=out_specs, check_vma=False
    )
```

profile of v0, /device:TPU:1, one launch (start us, length us, event | category | flops | bytes accessed | tf_op | source)
XLA Modules:
  0.0 1176.1 jit_solution(1637813087621144585)
XLA Ops:
  7.2 10.4 all_gather.15
  17.8 0.3 sub.40
  18.1 0.3 sub.41
  18.4 2.3 reduce-window.6
  20.7 0.3 slice_reduce_fusion
  21.7 0.2 fusion.5
  22.1 10.6 all_gather.16
  32.7 0.4 reshape.170
  33.3 0.6 gather_fusion
  34.0 3.0 convolution_bitcast_fusion
  37.0 9.7 scatter_custom_fusion
  46.7 14.6 %slice.22 = f32[1024,4608]{1,0:T(8,128)} slice(f32[1025,4608]{1,0:T(8,128)} %scatter_custom_fusion), slice={[0:1024], [0:4608]} | slice | bytes 37748736 | tf_op jit(solution)/shard_map/slice | solution.py:52
  61.4 18.7 %copy.22 = f32[1024,4608]{0,1:T(8,128)} copy(f32[1024,4608]{1,0:T(8,128)} %slice.22) | data formatting | bytes 37748736 | tf_op jit(solution)/shard_map/slice | solution.py:52
  80.0 22.9 %reshape.174 = f32[4,256,64,72]{1,0,3,2:T(4,128)} reshape(f32[1024,4608]{0,1:T(8,128)} %copy.22) | data formatting | bytes 37748736 | tf_op jit(solution)/shard_map/reshape | solution.py:56
  102.9 17.9 %copy.23 = f32[4,64,256,72]{2,3,1,0:T(8,128)} copy(f32[4,64,256,72]{2,0,3,1:T(4,128)} %bitcast.70) | data formatting | bytes 37748736 | tf_op jit(solution)/shard_map/transpose | solution.py:57
  120.9 452.5 %reduce-scatter.2.cloned.1.call-done = f32[1,256,72]{1,2,0:T(8,128)} async-done(((f32[256,256,72]{1,2,0:T(8,128)}), f32[1,256,72]{1,2,0:T(8,128)}) %reduce-scatter.2.cloned.1.call-update) | async-done | bytes 73744 | tf_op jit(solution)/shard_map/reduce_scatter | solution.py:60
  573.3 1.6 fusion.13
  575.0 0.7 all-reduce.5.cloned.1.call-update
  575.7 126.0 %all-gather.6.cloned.1.call-done = bf16[65536,72]{0,1:T(8,128)(2,1)} async-done(((bf16[256,72]{0,1:T(8,128)(2,1)}), bf16[65536,72]{0,1:T(8,128)(2,1)}) %all-gather.6.cloned.1.call-update) | async-done | bytes 9437200 | tf_op jit(solution)/shard_map/all_gather | solution.py:64
  701.7 9.8 copy.27
  711.5 13.4 %copy.24 = bf16[4,64,256,72]{2,0,3,1:T(4,128)(2,1)} copy(bf16[4,64,256,72]{2,1,0,3:T(8,128)(2,1)} %bitcast.71) | data formatting | bytes 18874368 | tf_op jit(solution)/shard_map/reshape | solution.py:66
  724.9 10.4 copy.28
  735.4 12.7 %copy.25 = bf16[1024,4608]{1,0:T(8,128)(2,1)} copy(bf16[1024,4608]{0,1:T(8,128)(2,1)} %bitcast.73) | data formatting | bytes 18874368 | tf_op jit(solution)/shard_map/reshape | solution.py:68
  748.1 8.0 concatenate.7
  756.1 6.4 gather_fusion.1
  762.6 4.3 fusion.4
  766.9 178.7 %all-reduce.5.cloned.1.call-done = s32[16384]{0:T(1024)} async-done(((s32[16384]{0:T(1024)}), s32[16384]{0:T(1024)}) %all-reduce.5.cloned.1.call-update) | async-done | bytes 65552
  945.6 0.9 and_select_fusion
  946.4 3.6 convolution_convert_fusion
  950.0 111.4 %all-gather.4.cloned.1.call-done = bf16[16384,64]{1,0:T(8,128)(2,1)} async-done(((bf16[64,64]{1,0:T(8,128)(2,1)}), bf16[16384,64]{1,0:T(8,128)(2,1)}) %all-gather.4.cloned.1.call-update) | async-done | bytes 2097168 | tf_op jit(solution)/shard_map/all_gather | solution.py:82
  1061.4 107.3 %scatter_custom_fusion.1 = f32[1025,64]{1,0:T(8,128)S(1)} fusion(s32[16384]{0:T(1024)S(1)} %and_select_fusion, bf16[16384,64]{1,0:T(8,128)(2,1)} %all-gather.4.cloned.1.call-done, f32[]{:T(128)} %constant.17.clone.1), kind=kCustom, calls=%fused_computation.6 | custom fusion | flops 2097152 | bytes 2359556 | tf_op jit(solution)/shard_map/scatter-add | solution.py:88
  1168.7 0.9 convert_element_type.33
  (27 shorter events, 1.5 us)
Async XLA Ops:
  7.2 566.2 %reduce-scatter.2.cloned.1.call-start = ((), (), s32[]{:S(2)}) async-start(), calls=%async_computation.1 | async-start | bytes 18948096 | tf_op jit(solution)/shard_map/reduce_scatter | solution.py:60
  22.1 24.7 %copy-start = (s32[16384]{0:T(1024)}, s32[16384]{0:T(1024)S(1)}, u32[]{:S(2)}) copy-start(s32[16384]{0:T(1024)S(1)} %get-tuple-element.5) | copy-start | bytes 196612
  120.8 452.5 %copy-start.1 = (bf16[256,72]{0,1:T(8,128)(2,1)S(1)}, bf16[256,72]{0,1:T(8,128)(2,1)}, u32[]{:S(2)}) copy-start(bf16[256,72]{0,1:T(8,128)(2,1)} %param.5) | copy-start | bytes 110596
  120.8 452.5 %copy-start.2 = (f32[72]{0:T(128)S(1)}, f32[72]{0:T(128)}, u32[]{:S(2)}) copy-start(f32[72]{0:T(128)} %param.9) | copy-start | bytes 868
  120.8 580.9 %all-gather.6.cloned.1.call-start = ((), (), s32[]{:S(2)}) async-start(), calls=%async_computation.3 | async-start | bytes 9474048 | tf_op jit(solution)/shard_map/all_gather | solution.py:64
  574.9 370.6 %all-reduce.5.cloned.1.call-start = ((), (), s32[]{:S(2)}) async-start(), calls=%async_computation.4 | async-start | bytes 131072
  575.7 485.7 %all-gather.4.cloned.1.call-start = ((), (), s32[]{:S(2)}) async-start(), calls=%async_computation.2 | async-start | bytes 4210688 | tf_op jit(solution)/shard_map/all_gather | solution.py:82
Sparse Core Ops, SparseCore 0:
  120.9 452.3 reduce-scatter.1
  578.3 123.3 all-gather.5
  708.7 236.8 all-reduce.4
  949.7 111.6 all-gather.3
where the time goes:
time: 1180 us
  waiting for transfers between devices  869 us (74%)
  local copies, waits for them, and re-layouts  138 us (12%)
  other arithmetic  123 us (10%)
  blocking collectives  21 us (2%)
  between operations  13.9 us (1%)
    reduce_scatter x1, waiting for transfers between devices, per_device(): lax.psum_scatter(arranged, ('dp', 'latent'), scatter_dimension=0, tiled=T...  452 us
    unnamed x5, waiting for transfers between devices  179 us
    all_gather x1, waiting for transfers between devices, per_device(): lax.all_gather(recon_error[None], ('dp', 'latent'), axis=0, tiled=True)  126 us
    all_gather x1, waiting for transfers between devices, per_device(): lax.all_gather(slot_code_grad, ('dp', 'latent'), axis=0, tiled=True)  111 us
    scatter-add x1, other arithmetic, per_device(): jax.ops.segment_sum(every_grad.astype(jnp.float32), target, num_segments=...  107 us
    slice x2, local copies, waits for them, and re-layouts, per_device(): jax.ops.segment_sum(partial_value, slot_token, num_segments=total_tokens...  33.3 us
  transfers between devices with their start and end apart: 4, of which 4 were waited for; matrix products, arithmetic and copies ran while one was open for 6% of the time, Pallas kernels for 0%

commit v1 on v0

v1 whole, which is shorter than its diff:
```python
import functools
import math

import jax
import jax.numpy as jnp
from jax import lax
from jax.experimental import pallas as pl
from jax.experimental.pallas import tpu as pltpu
from jax.sharding import PartitionSpec as P

MESH = pl.DeviceIdType.MESH
F32 = jnp.float32
BF16 = jnp.bfloat16
LAT_BLOCK = 64
BLK_DEV = 8
K_BLK = 4
MOST = 8
SLOTS = BLK_DEV * MOST
LATS = BLK_DEV * LAT_BLOCK
CODES = K_BLK * LAT_BLOCK


def dot(a, b, ca=1, cb=0):
    return lax.dot_general(a, b, (((ca,), (cb,)), ((), ())), preferred_element_type=F32)


def onehot(place, rows, first=0):
    ids = lax.broadcasted_iota(jnp.int32, (rows, place.shape[1]), 0) + first
    return jnp.where(ids == place, 1.0, 0.0).astype(BF16)


def exchange_kernel(
    X, Z, J, cap,
    ab_ref, codes_ref, act_ref, bias_ref, dec_hbm,
    recon_ref, rows_ref, own_ref, grad_ref, load_ref,
    dec, ab_all, place, c_all, q_all, zt, ecodes, codes_out, codes_in,
    part, a_out, a_in, gpt, b_out, b_in, dense, x_out, x_in, recon_all,
    b2_out, b2_in, a2_out, a2_in, yt, w_out, w_in, d_in, dense2, x2_out, x2_in, g_in,
    send_sem, recv_sem, dec_sem,
):
    T = ab_ref.shape[1]
    NT = X * T
    cw = act_ref.shape[1]
    span = Z * cw
    cs = CODES // J
    D = rows_ref.shape[1]
    d = lax.axis_index("dp")
    lat = lax.axis_index("latent")
    z = lax.div(lat, J)
    j = lax.rem(lat, J)

    def x_dev(i):
        return (i, lat)

    def z_dev(i):
        return (d, i * J + j)

    def j_dev(i):
        return (d, z * J + i)

    def to(me, n, r):
        return lax.rem(me + r, n)

    def frm(me, n, r):
        return lax.rem(me + n - r, n)

    load_dec = pltpu.make_async_copy(dec_hbm, dec, dec_sem)
    load_dec.start()

    barrier = pltpu.get_barrier_semaphore()
    peers = (
        [x_dev(to(d, X, r)) for r in range(1, X)]
        + [z_dev(to(z, Z, r)) for r in range(1, Z)]
        + [j_dev(to(j, J, r)) for r in range(1, J)]
    )
    for peer in peers:
        pl.semaphore_signal(barrier, inc=1, device_id=peer, device_id_type=MESH)
    pl.semaphore_wait(barrier, len(peers))

    sent = []

    def put(src, dst, device):
        at = len(sent)
        copy = pltpu.make_async_remote_copy(
            src_ref=src,
            dst_ref=dst,
            send_sem=send_sem.at[at],
            recv_sem=recv_sem.at[at],
            device_id=device,
            device_id_type=MESH,
        )
        copy.start()
        sent.append(copy)
        return copy

    ab_all[d] = ab_ref[...]
    copies = [put(ab_ref, ab_all.at[d], x_dev(to(d, X, r))) for r in range(1, X)]
    for copy in copies:
        copy.wait_recv()
    ab = jnp.concatenate([ab_all[i] for i in range(X)], axis=1)
    owner = ab >> int(math.log2(BLK_DEV))
    group = owner >> int(math.log2(J))

    def member(key, ids):
        named = key[0:1] == ids
        for k in range(1, K_BLK):
            named = named | (key[k : k + 1] == ids)
        return jnp.where(named, 1.0, 0.0)

    def column(n):
        return lax.broadcasted_iota(jnp.int32, (n, 1), 0)

    counts = jnp.sum(member(group, column(X * Z)), axis=1, keepdims=True)
    load_ref[...] = jnp.broadcast_to(
        jnp.max(counts, axis=0, keepdims=True), load_ref.shape
    ).astype(jnp.int32)

    pad = (-X) % 8
    row = column(X + pad)
    mem = jnp.concatenate(
        [
            member(owner, (row * Z + z) * J + j),
            member(owner, (d * Z + z) * J + column(J)),
            member(group, d * Z + column(Z)),
        ],
        axis=0,
    )
    lanes = min(128, NT)
    chunks = NT // lanes
    upto = jnp.where(
        lax.broadcasted_iota(jnp.int32, (lanes, lanes), 0)
        <= lax.broadcasted_iota(jnp.int32, (lanes, lanes), 1),
        1.0,
        0.0,
    ).astype(BF16)
    n_rows = mem.shape[0]
    stacked = jnp.concatenate(
        [mem[:, c * lanes : (c + 1) * lanes] for c in range(chunks)], axis=0
    )
    run = dot(stacked.astype(BF16), upto)
    base = jnp.zeros((n_rows, 1), F32)
    for c in range(chunks):
        here = run[c * n_rows : (c + 1) * n_rows]
        named = stacked[c * n_rows : (c + 1) * n_rows]
        place[:, c * lanes : (c + 1) * lanes] = jnp.where(
            named > 0.5, here - 1.0 + base, -1.0
        ).astype(jnp.int32)
        base = base + here[:, lanes - 1 : lanes]
    own_j = X + pad
    own_z = X + pad + J

    codes = codes_ref[...]
    for i in range(X):
        pick = onehot(place[i : i + 1, pl.ds(pl.multiple_of(d * T, T), T)], SLOTS)
        codes_out[i] = dot(pick, codes).astype(BF16)
    copies = []
    for r in range(1, X):
        i = to(d, X, r)
        copies.append(put(codes_out.at[i], codes_in.at[d], x_dev(i)))
    codes_in[d] = codes_out[d]

    def fill_q(i, carry):
        q_all[i] = onehot(place[pl.ds(own_j + i, 1), :], SLOTS)
        return carry

    lax.fori_loop(0, J, fill_q, 0)
    step = min(64, cap)
    per = cap // step

    def fill_c(n, carry):
        i = lax.div(n, per)
        first = pl.multiple_of(lax.rem(n, per) * step, step)
        c_all[i, pl.ds(first, step), :] = onehot(
            place[pl.ds(own_z + i, 1), :], step, first
        )
        return carry

    me = (d * Z + z) * J + j
    named = jnp.where(owner == me, (ab & (BLK_DEV - 1)) + 1, 0).astype(F32).astype(BF16)
    own_q = q_all[j]
    by_row = dot(own_q, named, 1, 1)
    by_col = dot(named, own_q, 1, 1)

    for copy in copies:
        copy.wait_recv()
    mine = codes_in[0].astype(F32)
    for i in range(1, X):
        mine = mine + codes_in[i].astype(F32)
    half = lax.broadcasted_iota(jnp.int32, (SLOTS, 2 * LAT_BLOCK), 1) >= LAT_BLOCK
    wide = []
    for k in range(K_BLK):
        one = mine[:, k * LAT_BLOCK : (k + 1) * LAT_BLOCK]
        wide.append(jnp.concatenate([one, one], axis=1))
    for m in range(BLK_DEV // 2):
        target = jnp.where(half, 2.0 * m + 2.0, 2.0 * m + 1.0)
        total = jnp.zeros((SLOTS, 2 * LAT_BLOCK), F32)
        for k in range(K_BLK):
            total = total + jnp.where(by_row[:, k : k + 1] == target, wide[k], 0.0)
        own_ref[:, m * 2 * LAT_BLOCK : (m + 1) * 2 * LAT_BLOCK] = total.astype(BF16)

    load_dec.wait()
    tile = 512 if D % 512 == 0 else D
    own = own_ref[...]

    def reconstruct(n, carry):
        at = pl.ds(pl.multiple_of(n * tile, tile), tile)
        part[:, at] = dot(own, dec[:, at])
        return carry

    lax.fori_loop(0, D // tile, reconstruct, 0)
    for i in range(J):
        a_out[i] = jnp.concatenate(
            [part[:, (n * J + i) * cw : (n * J + i + 1) * cw] for n in range(Z)], axis=1
        ).astype(BF16)
    copies = []
    for r in range(1, J):
        i = to(j, J, r)
        copies.append(put(a_out.at[i], a_in.at[j], j_dev(i)))
    a_in[j] = a_out[j]
    lax.fori_loop(0, Z * per, fill_c, 0)

    def fill_z(i, carry):
        zt[pl.ds(pl.multiple_of(i * SLOTS, SLOTS), SLOTS), :] = dot(
            q_all[i], c_all[z], 1, 1
        ).astype(BF16)
        return carry

    lax.fori_loop(0, J, fill_z, 0)
    for copy in copies:
        copy.wait_recv()

    arrived = a_in[...].reshape(J * SLOTS, span)
    gpt[...] = dot(arrived, zt[...], 0, 0)
    for n in range(Z):
        b_out[n] = gpt[n * cw : (n + 1) * cw, :].astype(BF16)
    copies = []
    for r in range(1, Z):
        i = to(z, Z, r)
        copies.append(put(b_out.at[i], b_in.at[z], z_dev(i)))
    b_in[z] = b_out[z]
    dense[...] = dot(b_in[z], c_all[z])
    for r in range(1, Z):
        copies[r - 1].wait_recv()
        i = frm(z, Z, r)
        dense[...] += dot(b_in[i], c_all[i])
    for i in range(X):
        x_out[i] = dense[:, i * T : (i + 1) * T]
    copies = []
    for r in range(1, X):
        i = to(d, X, r)
        copies.append(put(x_out.at[i], x_in.at[d], x_dev(i)))
    total = (bias_ref[...] - act_ref[...].astype(F32)).T + x_out[d]
    for r in range(1, X):
        copies[r - 1].wait_recv()
        total = total + x_in[frm(d, X, r)]
    recon = total.astype(BF16)
    recon_ref[...] = recon
    recon_all[d] = recon
    copies = [put(recon_ref, recon_all.at[d], x_dev(to(d, X, r))) for r in range(1, X)]
    for copy in copies:
        copy.wait_recv()

    whole = jnp.concatenate([recon_all[i] for i in range(X)], axis=1)
    copies = []
    for r in range(1, Z):
        i = to(z, Z, r)
        b2_out[i] = dot(whole, c_all[i], 1, 1).astype(BF16)
        copies.append(put(b2_out.at[i], b2_in.at[z], z_dev(i)))
    b2_in[z] = dot(whole, c_all[z], 1, 1).astype(BF16)
    for copy in copies:
        copy.wait_recv()
    flat = b2_in[...].astype(F32).reshape(span, cap).astype(BF16)
    a2_out[...] = dot(zt[...], flat, 1, 1).astype(BF16).reshape(J, SLOTS, span)
    copies = []
    for r in range(1, J):
        i = to(j, J, r)
        copies.append(put(a2_out.at[i], a2_in.at[j], j_dev(i)))
    a2_in[j] = a2_out[j]
    for copy in copies:
        copy.wait_recv()
    for m in range(Z // 2):
        pieces = [
            a2_in[i, :, n * cw : (n + 1) * cw].astype(F32)
            for n in (2 * m, 2 * m + 1)
            for i in range(J)
        ]
        width = 2 * J * cw
        rows_ref[:, m * width : (m + 1) * width] = jnp.concatenate(pieces, axis=1).astype(BF16)

    yt[...] = jnp.zeros_like(yt)

    def back(n, carry):
        at = pl.ds(pl.multiple_of(n * tile, tile), tile)
        yt[...] += dot(dec[:, at], rows_ref[:, at], 1, 1)
        return carry

    lax.fori_loop(0, D // tile, back, 0)
    for k in range(K_BLK):
        total = jnp.zeros((LAT_BLOCK, SLOTS), F32)
        for b in range(BLK_DEV):
            total = total + jnp.where(
                by_col[k : k + 1, :] == b + 1.0, yt[b * LAT_BLOCK : (b + 1) * LAT_BLOCK, :], 0.0
            )
        total = total.astype(BF16)
        for n in range(LAT_BLOCK // cs):
            w_out[k * (LAT_BLOCK // cs) + n] = total[n * cs : (n + 1) * cs]
    copies = []
    for r in range(1, J):
        i = to(j, J, r)
        copies.append(put(w_out.at[i], w_in.at[j], j_dev(i)))
    w_in[j] = w_out[j]
    for copy in copies:
        copy.wait_recv()
    merged = dot(w_in[0], zt[0:SLOTS, :])
    for i in range(1, J):
        merged = merged + dot(w_in[i], zt[i * SLOTS : (i + 1) * SLOTS, :])
    d_in[z] = merged.astype(BF16)
    copies = []
    for r in range(1, Z):
        copies.append(put(d_in.at[z], d_in.at[z], z_dev(to(z, Z, r))))
    dense2[...] = dot(d_in[z], c_all[z])
    for r in range(1, Z):
        copies[r - 1].wait_recv()
        i = frm(z, Z, r)
        dense2[...] += dot(d_in[i], c_all[i])
    for i in range(X):
        x2_out[i] = dense2[:, i * T : (i + 1) * T].astype(BF16)
    copies = []
    for r in range(1, X):
        i = to(d, X, r)
        copies.append(put(x2_out.at[i], x2_in.at[d], x_dev(i)))
    total = x2_out[d].astype(F32)
    for r in range(1, X):
        copies[r - 1].wait_recv()
        total = total + x2_in[frm(d, X, r)].astype(F32)
    g_in[j] = total.astype(BF16)
    copies = []
    for r in range(1, J):
        copies.append(put(g_in.at[j], g_in.at[j], j_dev(to(j, J, r))))
    for copy in copies:
        copy.wait_recv()
    grad_ref[...] = g_in[...].reshape(CODES, T)
    for copy in sent:
        copy.wait_send()


def exchange(X, Z, J, cap, collective_id, ab, codes, act, bias, decoder):
    T, cw = act.shape
    D = decoder.shape[1]
    NT = X * T
    span = Z * cw
    cs = CODES // J
    n_copies = 5 * (X - 1) + 3 * (Z - 1) + 4 * (J - 1)
    vmem = pltpu.VMEM
    whole = pl.BlockSpec(memory_space=pltpu.VMEM)
    rows = X + (-X) % 8 + J + Z
    return pl.pallas_call(
        functools.partial(exchange_kernel, X, Z, J, cap),
        out_shape=(
            jax.ShapeDtypeStruct((cw, T), BF16),
            jax.ShapeDtypeStruct((SLOTS, D), BF16),
            jax.ShapeDtypeStruct((SLOTS, LATS), BF16),
            jax.ShapeDtypeStruct((CODES, T), BF16),
            jax.ShapeDtypeStruct((8, 128), jnp.int32),
        ),
        in_specs=[whole] * 4 + [pl.BlockSpec(memory_space=pl.ANY)],
        out_specs=[whole] * 5,
        scratch_shapes=[
            vmem((LATS, D), BF16),
            vmem((X, 8, T), jnp.int32),
            vmem((rows, NT), jnp.int32),
            vmem((Z, cap, NT), BF16),
            vmem((J, SLOTS, NT), BF16),
            vmem((J * SLOTS, cap), BF16),
            vmem((SLOTS, CODES), BF16),
            vmem((X, SLOTS, CODES), BF16),
            vmem((X, SLOTS, CODES), BF16),
            vmem((SLOTS, D), F32),
            vmem((J, SLOTS, span), BF16),
            vmem((J, SLOTS, span), BF16),
            vmem((span, cap), F32),
            vmem((Z, cw, cap), BF16),
            vmem((Z, cw, cap), BF16),
            vmem((cw, NT), F32),
            vmem((X, cw, T), F32),
            vmem((X, cw, T), F32),
            vmem((X, cw, T), BF16),
            vmem((Z, cw, cap), BF16),
            vmem((Z, cw, cap), BF16),
            vmem((J, SLOTS, span), BF16),
            vmem((J, SLOTS, span), BF16),
            vmem((LATS, SLOTS), F32),
            vmem((J, cs, SLOTS), BF16),
            vmem((J, cs, SLOTS), BF16),
            vmem((Z, cs, cap), BF16),
            vmem((cs, NT), F32),
            vmem((X, cs, T), BF16),
            vmem((X, cs, T), BF16),
            vmem((J, cs, T), BF16),
            pltpu.SemaphoreType.DMA((n_copies,)),
            pltpu.SemaphoreType.DMA((n_copies,)),
            pltpu.SemaphoreType.DMA,
        ],
        compiler_params=pltpu.CompilerParams(
            collective_id=collective_id,
            has_side_effects=True,
            vmem_limit_bytes=52 * 2**20,
        ),
        name="exchange",
    )(ab, codes, act, bias, decoder)


def per_device(J, activations, latent_codes, active_blocks, decoder, decoder_bias):
    X = lax.axis_size("dp")
    Z = lax.axis_size("latent") // J
    ab = jnp.pad(active_blocks.T, ((0, 8 - K_BLK), (0, 0)), constant_values=-1)
    cap = min(J * SLOTS, X * activations.shape[0])
    recon, rows, own, grad, load = exchange(
        X, Z, J, cap, 0, ab, latent_codes, activations, decoder_bias[None, :], decoder
    )
    decoder_grad = dot(own, rows, 0, 0).astype(BF16)
    return recon.T, decoder_grad, grad.T


def solution(mesh):
    in_specs = (
        P("dp", "latent"),
        P("dp", None),
        P("dp", None),
        P(("dp", "latent"), None),
        P("latent"),
    )
    out_specs = (P("dp", "latent"), P(("dp", "latent"), None), P("dp", None))
    J = 8 if mesh.shape["latent"] >= 16 else 4
    return jax.shard_map(
        functools.partial(per_device, J),
        mesh=mesh, in_specs=in_specs, out_specs=out_specs, check_vma=False,
    )
```

time: 1180 us -> 112 us (0.09)
  waiting for transfers between devices: 869 us -> 0 us
  local copies, waits for them, and re-layouts: 138 us -> 4.5 us
  other arithmetic: 123 us -> 0 us
  Pallas kernels: 0 us -> 104 us
  blocking collectives: 21 us -> 0 us
  between operations: 13.9 us -> 0.65 us
    reduce_scatter x1 -> x0, waiting for transfers between devices: 452 us -> none  [per_device(): lax.psum_scatter(arranged, ('dp', 'latent'), scatter_dimension=0, tiled=T...]
    all_gather x2 -> x0, waiting for transfers between devices: 237 us -> none  [the longest x1 126 us: per_device(): lax.all_gather(recon_error[None], ('dp', 'latent'), axis=0, tiled=True)]
    unnamed x5 -> x0, waiting for transfers between devices: 179 us -> none
    scatter-add x2 -> x0, other arithmetic: 117 us -> none  [the longest x1 107 us: per_device(): jax.ops.segment_sum(every_grad.astype(jnp.float32), target, num_segments=...]
    pallas_call x0 -> x1, Pallas kernels: none -> 104 us  [exchange(): pl.pallas_call(functools.partial(exchange_kernel, X, Z, J, cap), out_shap...]
    reshape x4 -> x0, local copies, waits for them, and re-layouts: 49.5 us -> none  [the longest x1 22.9 us: per_device(): dense.reshape(dp_count, tok_dev, lat_count, col_width).transpose(0, 2, 1, 3)]
    slice x4 -> x0, local copies, waits for them, and re-layouts: 33.6 us -> none  [the longest x2 33.3 us: per_device(): jax.ops.segment_sum(partial_value, slot_token, num_segments=total_tokens...]
    all_gather x2 -> x0, blocking collectives: 21 us -> none  [the longest x1 10.6 us: per_device(): lax.all_gather(latent_codes, 'dp', axis=0, tiled=True)]
  transfers between devices with their start and end apart: 4 -> 0, of which waited for: 4 -> 0; matrix products, arithmetic and copies ran while one was open for 6% -> 0% of each run, Pallas kernels for 0% -> 0%
where the time goes in v1:
time: 112 us
  Pallas kernels  104 us (93%)
  local copies, waits for them, and re-layouts  4.5 us (4%)
  matrix products  3.6 us (3%)
    pallas_call x1, Pallas kernels, exchange(): pl.pallas_call(functools.partial(exchange_kernel, X, Z, J, cap), out_shap...  104 us
    unnamed x7, local copies, waits for them, and re-layouts  3.81 us
    dot_general x1, matrix products, dot(): lax.dot_general(a, b, (((ca,), (cb,)), ((), ())), preferred_element_type=...  3.6 us

profile of v1, /device:TPU:1, one launch (start us, length us, event | category | flops | bytes accessed | tf_op | source)
XLA Modules:
  0.0 112.3 jit_solution(7331447527450954311)
XLA Ops:
  0.6 0.7 pad.4.ab_ref
  1.3 0.9 copy.8.act_ref
  2.2 0.0 copy-start
  2.2 0.9 copy-done
  3.1 0.0 copy-start.1
  3.1 0.7 copy-done.1
  3.8 103.5 %exchange.1 = (bf16[72,256]{1,0:T(8,128)(2,1)S(1)}, bf16[64,4608]{1,0:T(8,128)(2,1)S(1)}, bf16[64,512]{1,0:T(8,128)(2,1)S(1)}, bf16[256,256]{1,0:T(8,128)(2,1)S(1)}, s32[8,128]{1,0:T(8,128)}) custom-call(s32[8,256]{1,0:T(8,128)S(1)} %pad.4.ab_ref, bf16[256,256]{1,0:T(8,128)(2,1)S(1)} %copy-done, bf16[256,72]{1,0:T(8,128)(2,1)S(1)} %copy.8.act_ref, ...), custom_call_target="tpu_custom_call" | custom-call | tf_op jit(solution)/shard_map/exchange/pallas_call | solution.py:357
  107.3 0.8 copy.9
  108.1 3.6 %convolution_convert_fusion = bf16[512,4608]{1,0:T(8,128)(2,1)} fusion(bf16[64,512]{1,0:T(8,128)(2,1)S(1)} %get-tuple-element.8, bf16[64,4608]{1,0:T(8,128)(2,1)S(1)} %get-tuple-element.9), kind=kOutput, calls=%fused_computation | convolution fusion | flops 304349184 | bytes 5373952 | tf_op jit(solution)/shard_map/dot_general | solution.py:24
  111.7 0.6 copy.11
Async XLA Ops:
  2.2 0.9 copy-start
  3.1 0.7 copy-start.1

commit v2 on v1

v2 whole, which is shorter than its diff:
```python
import functools
import math

import jax
import jax.numpy as jnp
from jax import lax
from jax.experimental import pallas as pl
from jax.experimental.pallas import tpu as pltpu
from jax.sharding import PartitionSpec as P

MESH = pl.DeviceIdType.MESH
F32 = jnp.float32
BF16 = jnp.bfloat16
LAT_BLOCK = 64
BLK_DEV = 8
K_BLK = 4
MOST = 8
MOST_DEV = BLK_DEV * MOST
LATS = BLK_DEV * LAT_BLOCK
CODES = K_BLK * LAT_BLOCK


def dot(a, b, ca=1, cb=0):
    return lax.dot_general(a, b, (((ca,), (cb,)), ((), ())), preferred_element_type=F32)


def iota(shape, axis):
    return lax.broadcasted_iota(jnp.int32, shape, axis)


def ones(where):
    return jnp.where(where, 1.0, 0.0)


def onehot(place, rows):
    return ones(iota((rows, place.shape[1]), 0) == place).astype(BF16)


def onehot_twice(place, rows, pack):
    ids = iota((rows * pack, place.shape[1]), 0)
    if pack == 2:
        ids = jnp.where(ids >= rows, ids - rows, ids)
    return ones(ids == place).astype(BF16)


def member(key, ids):
    named = key[0:1] == ids
    for k in range(1, K_BLK):
        named = named | (key[k : k + 1] == ids)
    return ones(named)


def exchange_kernel(
    X, Z, J, slots, cell,
    ab_hbm, codes_hbm, act_hbm, bias_hbm, dec_hbm,
    recon_ref, rows_ref, own_ref, grad_ref, over_ref,
    ab_my, codes, act, bias, dec, ab_all, c_all, q_all, zt, places, codes_out, codes_in,
    part, a_out, a_in, gpt, b_out, b_in, packed, recon_bf, b2_out, b2_in,
    a2_out, a2_in, yt, w_out, w_in, d_out, d_in, packed_d, g_in,
    send_sem, recv_sem, in_sem,
):
    T = ab_my.shape[1]
    NT = X * T
    G = X * Z
    pack = 128 // cell if cell < 128 else 1
    wide = cell * pack
    cw = act.shape[0]
    span = Z * cw
    cs = CODES // J
    D = dec.shape[1]
    top = b_out.shape[1]
    top_d = d_out.shape[1]
    d = lax.axis_index("dp")
    lat = lax.axis_index("latent")
    z = lax.div(lat, J)
    j = lax.rem(lat, J)
    g = d * Z + z

    def to(me, n, r):
        return lax.rem(me + r, n)

    def frm(me, n, r):
        return lax.rem(me + n - r, n)

    def near(n, r):
        return min(r, n - r)

    loads = [
        pltpu.make_async_copy(src, dst, in_sem.at[n])
        for n, (src, dst) in enumerate(
            ((ab_hbm, ab_my), (codes_hbm, codes), (act_hbm, act), (bias_hbm, bias), (dec_hbm, dec))
        )
    ]
    for load in loads:
        load.start()

    x_steps = sorted(range(1, X), key=lambda r: -near(X, r))
    j_steps = sorted(range(1, J), key=lambda r: -near(J, r))
    xz_steps = sorted(
        [(a, b) for a in range(X) for b in range(Z) if a + b > 0],
        key=lambda s: -near(X, s[0]) - near(Z, s[1]),
    )
    x_peers = [(to(d, X, r), lat) for r in x_steps]
    j_peers = [(d, z * J + to(j, J, r)) for r in j_steps]
    xz_peers = [(to(d, X, a), to(z, Z, b) * J + j) for a, b in xz_steps]
    barrier = pltpu.get_barrier_semaphore()
    for peer in j_peers + xz_peers:
        pl.semaphore_signal(barrier, inc=1, device_id=peer, device_id_type=MESH)

    sent = []

    def put(src, dst, device):
        at = len(sent)
        copy = pltpu.make_async_remote_copy(
            src_ref=src,
            dst_ref=dst,
            send_sem=send_sem.at[at],
            recv_sem=recv_sem.at[at],
            device_id=device,
            device_id_type=MESH,
        )
        copy.start()
        sent.append(copy)
        return copy

    lanes = min(128, T)
    per = T // lanes
    upto = ones(iota((lanes, lanes), 0) <= iota((lanes, lanes), 1)).astype(BF16)

    def running(mem):
        n = mem.shape[0]
        chunks = mem.shape[1] // lanes
        stacked = jnp.concatenate(
            [mem[:, c * lanes : (c + 1) * lanes] for c in range(chunks)], axis=0
        )
        run = dot(stacked.astype(BF16), upto)
        return [run[c * n : (c + 1) * n] for c in range(chunks)]

    def placed(mem, run, restart):
        pieces = []
        base = jnp.zeros((mem.shape[0], 1), F32)
        for c, here in enumerate(run):
            if c % restart == 0:
                base = jnp.zeros_like(base)
            named = mem[:, c * lanes : (c + 1) * lanes]
            pieces.append(jnp.where(named > 0.5, here - 1.0 + base, -1.0))
            base = base + here[:, lanes - 1 : lanes]
        return jnp.concatenate(pieces, axis=1).astype(jnp.int32)

    to_owner = int(math.log2(BLK_DEV))
    to_group = int(math.log2(J))
    for load in loads[:2]:
        load.wait()
    ab_here = ab_my[...]
    owner_here = ab_here >> to_owner
    pad_x = X + (-X) % 8
    mem = jnp.concatenate(
        [
            member(owner_here >> to_group, iota((G, 1), 0)),
            member(owner_here, (iota((pad_x, 1), 0) * Z + z) * J + j),
        ],
        axis=0,
    )
    places[...] = placed(mem, running(mem), per)
    for i in range(X):
        pick = onehot(places[G + i : G + i + 1, :], slots)
        codes_out[i] = dot(pick, codes[...]).astype(BF16)
    ab_all[d] = ab_here
    codes_in[d] = codes_out[d]
    pl.semaphore_wait(barrier, len(j_peers) + len(xz_peers))

    copies = []
    for r, peer in zip(x_steps, x_peers):
        copies.append(put(ab_my, ab_all.at[d], peer))
        copies.append(put(codes_out.at[to(d, X, r)], codes_in.at[d], peer))

    def fill_c(i, carry):
        c_all[i] = onehot_twice(places[pl.ds(i, 1), :], cell, pack)
        return carry

    lax.fori_loop(0, G, fill_c, 0)
    loads[2].wait()
    loads[3].wait()
    column = jnp.broadcast_to(bias[...], (8, cw)).T[:, 0:1]
    offset = column - act[...].astype(F32)
    for copy in copies:
        copy.wait_recv()

    ab = jnp.concatenate([ab_all[i] for i in range(X)], axis=1)
    owner = ab >> to_owner
    group = owner >> to_group
    mem_j = member(owner, g * J + iota((J + (-J) % 8, 1), 0))
    mem_own = member(owner, g * J + j + 0 * iota((8, 1), 0))
    mem_group = member(group, g + 0 * iota((8, 1), 0))
    n_j = mem_j.shape[0]
    mem = jnp.concatenate([mem_j, mem_own, mem_group], axis=0)
    run = running(mem)
    in_owner = placed(mem, run, NT // lanes)
    anew = placed(mem, run, per)
    for i in range(J):
        q_all[i] = onehot(in_owner[i : i + 1], slots)
    own_q = q_all[j]
    named = jnp.where(owner == g * J + j, (ab & (BLK_DEV - 1)) + 1, 0)
    named = jnp.concatenate([named.astype(F32), jnp.zeros((8 - K_BLK, NT), F32)], axis=0)
    named = named.astype(BF16)
    by_row = dot(own_q, named, 1, 1)
    by_col = dot(named, own_q, 1, 1)
    mine = jnp.zeros((slots, CODES), F32)
    for i in range(X):
        at = slice(i * T, (i + 1) * T)
        pick = onehot(anew[n_j : n_j + 1, at], slots)
        mine = mine + dot(dot(own_q[:, at], pick, 1, 1).astype(BF16), codes_in[i])
    half = iota((slots, 2 * LAT_BLOCK), 1) >= LAT_BLOCK
    twice = []
    for k in range(K_BLK):
        one = mine[:, k * LAT_BLOCK : (k + 1) * LAT_BLOCK]
        twice.append(jnp.concatenate([one, one], axis=1))
    for m in range(BLK_DEV // 2):
        target = jnp.where(half, 2.0 * m + 2.0, 2.0 * m + 1.0)
        total = jnp.zeros((slots, 2 * LAT_BLOCK), F32)
        for k in range(K_BLK):
            total = total + jnp.where(by_row[:, k : k + 1] == target, twice[k], 0.0)
        own_ref[:, m * 2 * LAT_BLOCK : (m + 1) * 2 * LAT_BLOCK] = total.astype(BF16)

    loads[4].wait()
    tile = 512 if D % 512 == 0 else D
    own = own_ref[...]

    def reconstruct(n, carry):
        at = pl.ds(pl.multiple_of(n * tile, tile), tile)
        part[:, at] = dot(own, dec[:, at])
        return carry

    lax.fori_loop(0, D // tile, reconstruct, 0)
    for i in range(J):
        a_out[i] = jnp.concatenate(
            [part[:, (n * J + i) * cw : (n * J + i + 1) * cw] for n in range(Z)], axis=1
        ).astype(BF16)
    copies = []
    for r, peer in zip(j_steps, j_peers):
        copies.append(put(a_out.at[to(j, J, r)], a_in.at[j], peer))
    a_in[j] = a_out[j]
    for i in range(X):
        at = slice(i * T, (i + 1) * T)
        pick = onehot_twice(anew[n_j + 8 : n_j + 9, at], cell, pack)
        zt[:, i * wide : (i + 1) * wide] = dot(
            q_all[...].reshape(J * slots, NT)[:, at], pick, 1, 1
        ).astype(BF16)
    over = jnp.zeros((1, 1), F32)
    for i in range(G * J // 64):
        count = jnp.sum(member(owner, i * 64 + iota((64, 1), 0)), axis=1, keepdims=True)
        over = over + jnp.max(ones(count > slots), axis=0, keepdims=True)
    count = member(group, iota((G, 1), 0))
    for i in range(X):
        here = jnp.sum(count[:, i * T : (i + 1) * T], axis=1, keepdims=True)
        over = over + jnp.max(ones(here > cell), axis=0, keepdims=True)
    over_ref[...] = jnp.broadcast_to(over, over_ref.shape).astype(jnp.int32)
    for copy in copies:
        copy.wait_recv()

    left = lax.rem(iota((8, wide), 1), 128) < 64
    left_row = left[0:1]

    def packs(x, rows):
        if pack == 1:
            return x
        rest = x[rows:]
        if rest.shape[0] < rows:
            rest = jnp.concatenate([rest, rest[: rows - rest.shape[0]]], axis=0)
        return jnp.where(left_row, x[:rows], rest)

    def unpacks(x, rows):
        if pack == 1:
            return x
        x = x.astype(F32)
        first = jnp.where(left_row, x, 0.0)
        rest = jnp.where(left_row, 0.0, x[: rows - x.shape[0]])
        return jnp.concatenate([first, rest], axis=0).astype(BF16)

    arrived = a_in[...].reshape(J * slots, span)
    gpt[...] = dot(arrived, zt[...], 0, 0)
    for i in range(X):
        for n in range(Z):
            b_out[i * Z + n] = packs(
                gpt[n * cw : (n + 1) * cw, i * wide : (i + 1) * wide], top
            ).astype(BF16)
    copies = []
    for (a, b), peer in zip(xz_steps, xz_peers):
        copies.append(put(b_out.at[to(d, X, a) * Z + to(z, Z, b)], b_in.at[g], peer))
    b_in[g] = b_out[g]
    for copy in copies:
        copy.wait_recv()
    for i in range(G):
        packed[:, i * wide : (i + 1) * wide] = unpacks(b_in[i], cw)
    flat_c = c_all[...].reshape(G * wide, T)
    recon = (dot(packed[...], flat_c) + offset).astype(BF16)
    recon_ref[...] = recon
    recon_bf[...] = recon

    copies = []
    for a in sorted(range(X), key=lambda r: -near(X, r)):
        x = to(d, X, a)
        back_c = c_all[pl.ds(x * Z, Z)].reshape(Z * wide, T)
        sends = dot(recon_bf[...], back_c, 1, 1)
        for n in range(Z):
            b2_out[x * Z + n] = packs(sends[:, n * wide : (n + 1) * wide], top).astype(BF16)
        for (a2, b), peer in zip(xz_steps, xz_peers):
            if a2 == a:
                copies.append(put(b2_out.at[x * Z + to(z, Z, b)], b2_in.at[g], peer))
    b2_in[g] = b2_out[g]
    for copy in copies:
        copy.wait_recv()
    pieces = []
    for n in range(Z):
        pieces.append(
            jnp.concatenate([unpacks(b2_in[i * Z + n], cw) for i in range(X)], axis=1).astype(F32)
        )
    flat = jnp.concatenate(pieces, axis=0).astype(BF16)
    a2_out[...] = dot(zt[...], flat, 1, 1).astype(BF16).reshape(J, slots, span)
    copies = []
    for r, peer in zip(j_steps, j_peers):
        copies.append(put(a2_out.at[to(j, J, r)], a2_in.at[j], peer))
    a2_in[j] = a2_out[j]
    for copy in copies:
        copy.wait_recv()
    for m in range(Z // 2):
        pieces = [
            a2_in[i, :, n * cw : (n + 1) * cw].astype(F32)
            for n in (2 * m, 2 * m + 1)
            for i in range(J)
        ]
        width = 2 * J * cw
        rows_ref[:, m * width : (m + 1) * width] = jnp.concatenate(pieces, axis=1).astype(BF16)

    yt[...] = jnp.zeros_like(yt)

    def back(n, carry):
        at = pl.ds(pl.multiple_of(n * tile, tile), tile)
        yt[...] += dot(dec[:, at], rows_ref[:, at], 1, 1)
        return carry

    lax.fori_loop(0, D // tile, back, 0)
    for k in range(K_BLK):
        total = jnp.zeros((LAT_BLOCK, slots), F32)
        for b in range(BLK_DEV):
            total = total + jnp.where(
                by_col[k : k + 1, :] == b + 1.0, yt[b * LAT_BLOCK : (b + 1) * LAT_BLOCK, :], 0.0
            )
        total = total.astype(BF16)
        for n in range(LAT_BLOCK // cs):
            w_out[k * (LAT_BLOCK // cs) + n] = total[n * cs : (n + 1) * cs]
    copies = []
    for r, peer in zip(j_steps, j_peers):
        copies.append(put(w_out.at[to(j, J, r)], w_in.at[j], peer))
    w_in[j] = w_out[j]
    for copy in copies:
        copy.wait_recv()
    merged = dot(w_in[0], zt[0:slots, :])
    for i in range(1, J):
        merged = merged + dot(w_in[i], zt[i * slots : (i + 1) * slots, :])
    for i in range(X):
        d_out[i] = packs(merged[:, i * wide : (i + 1) * wide], top_d).astype(BF16)
    copies = []
    for (a, b), peer in zip(xz_steps, xz_peers):
        copies.append(put(d_out.at[to(d, X, a)], d_in.at[g], peer))
    d_in[g] = d_out[d]
    for copy in copies:
        copy.wait_recv()
    for i in range(G):
        packed_d[:, i * wide : (i + 1) * wide] = unpacks(d_in[i], cs)
    g_in[j] = dot(packed_d[...], c_all[...].reshape(G * wide, T)).astype(BF16)
    copies = []
    for r, peer in zip(j_steps, j_peers):
        copies.append(put(g_in.at[j], g_in.at[j], peer))
    for copy in copies:
        copy.wait_recv()
    grad_ref[...] = g_in[...].reshape(CODES, T)
    for copy in sent:
        copy.wait_send()


def exchange(X, Z, J, slots, cell, collective_id, ab, codes, act, bias, decoder):
    cw, T = act.shape
    D = decoder.shape[1]
    NT = X * T
    G = X * Z
    span = Z * cw
    cs = CODES // J
    pack = 128 // cell if cell < 128 else 1
    wide = cell * pack
    top = cw if pack == 1 else -(-cw // 16) * 8
    top_d = cs if pack == 1 else cs // 2
    n_copies = 2 * (X - 1) + 3 * (G - 1) + 4 * (J - 1)
    vmem = pltpu.VMEM
    whole = pl.BlockSpec(memory_space=pltpu.VMEM)
    far = pl.BlockSpec(memory_space=pl.ANY)
    return pl.pallas_call(
        functools.partial(exchange_kernel, X, Z, J, slots, cell),
        out_shape=(
            jax.ShapeDtypeStruct((cw, T), BF16),
            jax.ShapeDtypeStruct((slots, D), BF16),
            jax.ShapeDtypeStruct((slots, LATS), BF16),
            jax.ShapeDtypeStruct((CODES, T), BF16),
            jax.ShapeDtypeStruct((8, 128), jnp.int32),
        ),
        in_specs=[far] * 5,
        out_specs=[whole] * 5,
        scratch_shapes=[
            vmem((K_BLK, T), jnp.int32),
            vmem((T, CODES), BF16),
            vmem((cw, T), BF16),
            vmem((1, cw), F32),
            vmem((LATS, D), BF16),
            vmem((X, K_BLK, T), jnp.int32),
            vmem((G, wide, T), BF16),
            vmem((J, slots, NT), BF16),
            vmem((J * slots, X * wide), BF16),
            vmem((G + X + (-X) % 8, T), jnp.int32),
            vmem((X, slots, CODES), BF16),
            vmem((X, slots, CODES), BF16),
            vmem((slots, D), F32),
            vmem((J, slots, span), BF16),
            vmem((J, slots, span), BF16),
            vmem((span, X * wide), F32),
            vmem((G, top, wide), BF16),
            vmem((G, top, wide), BF16),
            vmem((cw, G * wide), BF16),
            vmem((cw, T), BF16),
            vmem((G, top, wide), BF16),
            vmem((G, top, wide), BF16),
            vmem((J, slots, span), BF16),
            vmem((J, slots, span), BF16),
            vmem((LATS, slots), F32),
            vmem((J, cs, slots), BF16),
            vmem((J, cs, slots), BF16),
            vmem((X, top_d, wide), BF16),
            vmem((G, top_d, wide), BF16),
            vmem((cs, G * wide), BF16),
            vmem((J, cs, T), BF16),
            pltpu.SemaphoreType.DMA((n_copies,)),
            pltpu.SemaphoreType.DMA((n_copies,)),
            pltpu.SemaphoreType.DMA((5,)),
        ],
        compiler_params=pltpu.CompilerParams(
            collective_id=collective_id,
            has_side_effects=True,
            vmem_limit_bytes=52 * 2**20,
        ),
        name="exchange_%d_%d" % (slots, cell),
    )(ab, codes, act, bias, decoder)


def per_device(J, activations, latent_codes, active_blocks, decoder, decoder_bias):
    X = lax.axis_size("dp")
    Z = lax.axis_size("latent") // J
    T = activations.shape[0]
    args = (active_blocks.T, latent_codes, activations.T, decoder_bias[None, :], decoder)
    *fast, over = exchange(X, Z, J, 48, 64, 0, *args)

    def finish(recon, rows, own, grad):
        return recon.T, dot(own, rows, 0, 0).astype(BF16), grad.T

    def roomy():
        return finish(*exchange(X, Z, J, MOST_DEV, T, 1, *args)[:4])

    return lax.cond(over[0, 0] > 0, roomy, lambda: finish(*fast))


def solution(mesh):
    in_specs = (
        P("dp", "latent"),
        P("dp", None),
        P("dp", None),
        P(("dp", "latent"), None),
        P("latent"),
    )
    out_specs = (P("dp", "latent"), P(("dp", "latent"), None), P("dp", None))
    J = 8 if mesh.shape["latent"] >= 16 else 4
    return jax.shard_map(
        functools.partial(per_device, J),
        mesh=mesh, in_specs=in_specs, out_specs=out_specs, check_vma=False,
    )
```

time: 112 us -> 77.7 us (0.69)
  Pallas kernels: 104 us -> 71.8 us
  matrix products: 3.6 us -> 1.41 us
  local copies, waits for them, and re-layouts: 4.5 us -> 2.84 us
    pallas_call x1, Pallas kernels: 104 us -> 71.8 us  [exchange(): pl.pallas_call(functools.partial(exchange_kernel, X, Z, J, slots, cell),...]
    dot_general x1, matrix products: 3.6 us -> 1.41 us  [dot(): lax.dot_general(a, b, (((ca,), (cb,)), ((), ())), preferred_element_type=...]
    unnamed x7 -> x14, local copies, waits for them, and re-layouts: 3.81 us -> 2.23 us
where the time goes in v2:
time: 77.7 us; the launch traced here: 77.6 us
  Pallas kernels  71.8 us (92%)
  local copies, waits for them, and re-layouts  2.84 us (4%)
  matrix products  1.41 us (2%)
  between operations  1.39 us (2%)
    pallas_call x1, Pallas kernels, exchange(): pl.pallas_call(functools.partial(exchange_kernel, X, Z, J, slots, cell),...  71.8 us
    unnamed x14, local copies, waits for them, and re-layouts  2.23 us

profile of v2, /device:TPU:1, one launch (start us, length us, event | category | flops | bytes accessed | tf_op | source)
XLA Modules:
  0.0 77.6 jit_solution(14724253249309735611)
XLA Ops:
  0.6 0.0 copy-start.1
  0.6 0.0 copy-start.5
  0.7 0.0 copy-start.4
  0.7 0.0 copy-start.2
  0.7 71.8 %exchange_48_64.1 = (bf16[72,256]{1,0:T(8,128)(2,1)S(1)}, bf16[48,4608]{1,0:T(8,128)(2,1)S(1)}, bf16[48,512]{1,0:T(8,128)(2,1)S(1)}, bf16[256,256]{1,0:T(8,128)(2,1)S(1)}, s32[8,128]{1,0:T(8,128)S(1)}) custom-call(s32[4,256]{1,0:T(4,128)} %bitcast.18, bf16[256,256]{1,0:T(8,128)(2,1)} %codes_hbm.1, bf16[72,256]{1,0:T(8,128)(2,1)} %bitcast.13, ...), custom_call_target="tpu_custom_call" | custom-call | tf_op jit(solution)/shard_map/exchange_48_64/pallas_call | solution.py:397
  72.5 0.5 slice.3
  73.7 0.0 copy-done.1
  73.7 0.0 copy-done.5
  73.7 0.0 copy-done.4
  73.7 0.0 copy-done.2
  73.7 1.7 %conditional.2 = (bf16[256,72]{0,1:T(8,128)(2,1)S(1)}, bf16[512,4608]{1,0:T(8,128)(2,1)S(1)}, bf16[256,256]{1,0:T(8,128)(2,1)S(1)}) conditional(s32[]{:T(128)} %bitcast.7, (bf16[72,256]{1,0:T(8,128)(2,1)S(1)}, bf16[48,512]{1,0:T(8,128)(2,1)S(1)}, bf16[48,4608]{1,0:T(8,128)(2,1)S(1)}, bf16[256,256]{1,0:T(8,128)(2,1)S(1)}) %tuple.29, ...), branch_computations={%region_0.0_spmd, %region_1.0_spmd} | conditional | flops 301989888 | bytes 5636120
  73.7 0.1 copy.9
  73.8 1.4 %fusion = bf16[512,4608]{1,0:T(8,128)(2,1)S(1)} fusion(bf16[48,512]{1,0:T(8,128)(2,1)S(1)} %get-tuple-element.23, bf16[48,4608]{1,0:T(8,128)(2,1)S(1)} %get-tuple-element.24), kind=kOutput, calls=%fused_computation | convolution fusion | flops 226492416 | bytes 5210112 | tf_op jit(solution)/shard_map/cond/branch_0_fun/dot_general | solution.py:24
  75.4 0.0 copy-start
  75.4 0.0 copy-start.3
  75.4 0.7 copy.20
  76.1 1.5 %copy-done = bf16[512,4608]{1,0:T(8,128)(2,1)} copy-done((bf16[512,4608]{1,0:T(8,128)(2,1)}, bf16[512,4608]{1,0:T(8,128)(2,1)S(1)}, u32[]{:S(2)}) %copy-start) | copy-done | bytes 4718616
  77.6 0.0 copy-done.3
  (1 shorter events, 0.0 us)
Async XLA Ops:
  0.6 73.0 %copy-start.1 = (bf16[256,256]{1,0:T(8,128)(2,1)S(1)}, bf16[256,256]{1,0:T(8,128)(2,1)}, u32[]{:S(2)}) copy-start(bf16[256,256]{1,0:T(8,128)(2,1)} %codes_hbm.1) | copy-start | bytes 393220
  0.6 73.0 %copy-start.5 = (f32[72]{0:T(128)S(1)}, f32[72]{0:T(128)}, u32[]{:S(2)}) copy-start(f32[72]{0:T(128)} %param.11) | copy-start | bytes 868
  0.7 73.0 %copy-start.4 = (s32[256,4]{0,1:T(4,128)S(1)}, s32[256,4]{0,1:T(4,128)}, u32[]{:S(2)}) copy-start(s32[256,4]{0,1:T(4,128)} %param.9) | copy-start | bytes 12292
  0.7 73.0 %copy-start.2 = (bf16[256,72]{0,1:T(8,128)(2,1)S(1)}, bf16[256,72]{0,1:T(8,128)(2,1)}, u32[]{:S(2)}) copy-start(bf16[256,72]{0,1:T(8,128)(2,1)} %param.7) | copy-start | bytes 110596
  75.4 2.2 %copy-start = (bf16[512,4608]{1,0:T(8,128)(2,1)}, bf16[512,4608]{1,0:T(8,128)(2,1)S(1)}, u32[]{:S(2)}) copy-start(bf16[512,4608]{1,0:T(8,128)(2,1)S(1)} %get-tuple-element.76) | copy-start | bytes 14155780
  75.4 2.2 %copy-start.3 = (bf16[256,256]{1,0:T(8,128)(2,1)}, bf16[256,256]{1,0:T(8,128)(2,1)S(1)}, u32[]{:S(2)}) copy-start(bf16[256,256]{1,0:T(8,128)(2,1)S(1)} %get-tuple-element.77) | copy-start | bytes 393220

commit v3 on v2

--- a/solution.py
+++ b/solution.py
@@ -53,7 +53,7 @@
 def exchange_kernel(
     X, Z, J, slots, cell,
     ab_hbm, codes_hbm, act_hbm, bias_hbm, dec_hbm,
-    recon_ref, rows_ref, own_ref, grad_ref, over_ref,
+    recon_ref, rows, own, grad_ref, over_ref,
     ab_my, codes, act, bias, dec, ab_all, c_all, q_all, zt, places, codes_out, codes_in,
     part, a_out, a_in, gpt, b_out, b_in, packed, recon_bf, b2_out, b2_in,
     a2_out, a2_in, yt, w_out, w_in, d_out, d_in, packed_d, g_in,
@@ -153,18 +153,10 @@
         load.wait()
     ab_here = ab_my[...]
     owner_here = ab_here >> to_owner
-    pad_x = X + (-X) % 8
-    mem = jnp.concatenate(
-        [
-            member(owner_here >> to_group, iota((G, 1), 0)),
-            member(owner_here, (iota((pad_x, 1), 0) * Z + z) * J + j),
-        ],
-        axis=0,
-    )
-    places[...] = placed(mem, running(mem), per)
+    mem = member(owner_here, (iota((X + (-X) % 8, 1), 0) * Z + z) * J + j)
+    along = placed(mem, running(mem), per)
     for i in range(X):
-        pick = onehot(places[G + i : G + i + 1, :], slots)
-        codes_out[i] = dot(pick, codes[...]).astype(BF16)
+        codes_out[i] = dot(onehot(along[i : i + 1], slots), codes[...]).astype(BF16)
     ab_all[d] = ab_here
     codes_in[d] = codes_out[d]
     pl.semaphore_wait(barrier, len(j_peers) + len(xz_peers))
@@ -174,11 +166,8 @@
         copies.append(put(ab_my, ab_all.at[d], peer))
         copies.append(put(codes_out.at[to(d, X, r)], codes_in.at[d], peer))
 
-    def fill_c(i, carry):
-        c_all[i] = onehot_twice(places[pl.ds(i, 1), :], cell, pack)
-        return carry
-
-    lax.fori_loop(0, G, fill_c, 0)
+    mem = member(owner_here >> to_group, iota((G, 1), 0))
+    places[...] = placed(mem, running(mem), per)
     loads[2].wait()
     loads[3].wait()
     column = jnp.broadcast_to(bias[...], (8, cw)).T[:, 0:1]
@@ -220,26 +209,29 @@
         total = jnp.zeros((slots, 2 * LAT_BLOCK), F32)
         for k in range(K_BLK):
             total = total + jnp.where(by_row[:, k : k + 1] == target, twice[k], 0.0)
-        own_ref[:, m * 2 * LAT_BLOCK : (m + 1) * 2 * LAT_BLOCK] = total.astype(BF16)
+        own[:, m * 2 * LAT_BLOCK : (m + 1) * 2 * LAT_BLOCK] = total.astype(BF16)
 
     loads[4].wait()
     tile = 512 if D % 512 == 0 else D
-    own = own_ref[...]
-
-    def reconstruct(n, carry):
-        at = pl.ds(pl.multiple_of(n * tile, tile), tile)
-        part[:, at] = dot(own, dec[:, at])
-        return carry
-
-    lax.fori_loop(0, D // tile, reconstruct, 0)
+    own_codes = own[...]
+
+    for n in range(D // tile):
+        at = slice(n * tile, (n + 1) * tile)
+        part[:, at] = dot(own_codes, dec[:, at]).astype(BF16)
     for i in range(J):
         a_out[i] = jnp.concatenate(
             [part[:, (n * J + i) * cw : (n * J + i + 1) * cw] for n in range(Z)], axis=1
-        ).astype(BF16)
+        )
     copies = []
     for r, peer in zip(j_steps, j_peers):
         copies.append(put(a_out.at[to(j, J, r)], a_in.at[j], peer))
     a_in[j] = a_out[j]
+
+    def fill_c(i, carry):
+        c_all[i] = onehot_twice(places[pl.ds(i, 1), :], cell, pack)
+        return carry
+
+    lax.fori_loop(0, G, fill_c, 0)
     for i in range(X):
         at = slice(i * T, (i + 1) * T)
         pick = onehot_twice(anew[n_j + 8 : n_j + 9, at], cell, pack)
@@ -247,14 +239,15 @@
             q_all[...].reshape(J * slots, NT)[:, at], pick, 1, 1
         ).astype(BF16)
     over = jnp.zeros((1, 1), F32)
-    for i in range(G * J // 64):
-        count = jnp.sum(member(owner, i * 64 + iota((64, 1), 0)), axis=1, keepdims=True)
+    part_of = min(64, G * J)
+    for i in range(G * J // part_of):
+        count = jnp.sum(member(owner, i * part_of + iota((part_of, 1), 0)), axis=1, keepdims=True)
         over = over + jnp.max(ones(count > slots), axis=0, keepdims=True)
     count = member(group, iota((G, 1), 0))
     for i in range(X):
         here = jnp.sum(count[:, i * T : (i + 1) * T], axis=1, keepdims=True)
         over = over + jnp.max(ones(here > cell), axis=0, keepdims=True)
-    over_ref[...] = jnp.broadcast_to(over, over_ref.shape).astype(jnp.int32)
+    over_ref[0, 0] = jnp.max(over).astype(jnp.int32)
     for copy in copies:
         copy.wait_recv()
 
@@ -325,21 +318,14 @@
         copy.wait_recv()
     for m in range(Z // 2):
         pieces = [
-            a2_in[i, :, n * cw : (n + 1) * cw].astype(F32)
+            a2_in[i, :, n * cw : (n + 1) * cw]
             for n in (2 * m, 2 * m + 1)
             for i in range(J)
         ]
         width = 2 * J * cw
-        rows_ref[:, m * width : (m + 1) * width] = jnp.concatenate(pieces, axis=1).astype(BF16)
-
-    yt[...] = jnp.zeros_like(yt)
-
-    def back(n, carry):
-        at = pl.ds(pl.multiple_of(n * tile, tile), tile)
-        yt[...] += dot(dec[:, at], rows_ref[:, at], 1, 1)
-        return carry
-
-    lax.fori_loop(0, D // tile, back, 0)
+        rows[:, m * width : (m + 1) * width] = jnp.concatenate(pieces, axis=1)
+
+    yt[...] = dot(dec[...], rows[...], 1, 1)
     for k in range(K_BLK):
         total = jnp.zeros((LAT_BLOCK, slots), F32)
         for b in range(BLK_DEV):
@@ -401,10 +387,10 @@
             jax.ShapeDtypeStruct((slots, D), BF16),
             jax.ShapeDtypeStruct((slots, LATS), BF16),
             jax.ShapeDtypeStruct((CODES, T), BF16),
-            jax.ShapeDtypeStruct((8, 128), jnp.int32),
+            jax.ShapeDtypeStruct((1, 1), jnp.int32),
         ),
         in_specs=[far] * 5,
-        out_specs=[whole] * 5,
+        out_specs=[whole] * 4 + [pl.BlockSpec(memory_space=pltpu.SMEM)],
         scratch_shapes=[
             vmem((K_BLK, T), jnp.int32),
             vmem((T, CODES), BF16),
@@ -415,10 +401,10 @@
             vmem((G, wide, T), BF16),
             vmem((J, slots, NT), BF16),
             vmem((J * slots, X * wide), BF16),
-            vmem((G + X + (-X) % 8, T), jnp.int32),
+            vmem((G, T), jnp.int32),
             vmem((X, slots, CODES), BF16),
             vmem((X, slots, CODES), BF16),
-            vmem((slots, D), F32),
+            vmem((slots, D), BF16),
             vmem((J, slots, span), BF16),
             vmem((J, slots, span), BF16),
             vmem((span, X * wide), F32),
@@ -450,20 +436,62 @@
     )(ab, codes, act, bias, decoder)
 
 
+def finish_kernel(recon_in, rows_ref, own_ref, grad_in, recon_out, dgrad_ref, grad_out):
+    @pl.when(pl.program_id(0) == 0)
+    def _():
+        recon_out[...] = recon_in[...]
+        grad_out[...] = grad_in[...].T
+
+    dgrad_ref[...] = dot(own_ref[...], rows_ref[...], 0, 0).astype(BF16)
+
+
+def finish(recon, rows, own, grad):
+    slots, D = rows.shape
+    tile = 512 if D % 512 == 0 else D
+    CO, T = grad.shape
+
+    def fixed(shape):
+        return pl.BlockSpec(shape, lambda n: (0, 0))
+
+    recon, decoder_grad, grad = pl.pallas_call(
+        finish_kernel,
+        grid=(D // tile,),
+        out_shape=(
+            jax.ShapeDtypeStruct(recon.shape, BF16),
+            jax.ShapeDtypeStruct((LATS, D), BF16),
+            jax.ShapeDtypeStruct((T, CO), BF16),
+        ),
+        in_specs=[
+            fixed(recon.shape),
+            pl.BlockSpec((slots, tile), lambda n: (0, n)),
+            fixed(own.shape),
+            fixed(grad.shape),
+        ],
+        out_specs=[
+            fixed(recon.shape),
+            pl.BlockSpec((LATS, tile), lambda n: (0, n)),
+            fixed((T, CO)),
+        ],
+        cost_estimate=pl.CostEstimate(
+            flops=2 * slots * LATS * D, bytes_accessed=2 * LATS * D, transcendentals=0
+        ),
+        name="finish_%d" % slots,
+    )(recon, rows, own, grad)
+    return recon, decoder_grad, grad
+
+
 def per_device(J, activations, latent_codes, active_blocks, decoder, decoder_bias):
     X = lax.axis_size("dp")
     Z = lax.axis_size("latent") // J
     T = activations.shape[0]
     args = (active_blocks.T, latent_codes, activations.T, decoder_bias[None, :], decoder)
-    *fast, over = exchange(X, Z, J, 48, 64, 0, *args)
-
-    def finish(recon, rows, own, grad):
-        return recon.T, dot(own, rows, 0, 0).astype(BF16), grad.T
+    *fast, over = exchange(X, Z, J, 40, 64, 0, *args)
 
     def roomy():
         return finish(*exchange(X, Z, J, MOST_DEV, T, 1, *args)[:4])
 
-    return lax.cond(over[0, 0] > 0, roomy, lambda: finish(*fast))
+    recon, decoder_grad, grad = lax.cond(over[0, 0] > 0, roomy, lambda: finish(*fast))
+    return recon.T, decoder_grad, grad
 
 
 def solution(mesh):

time: 77.7 us -> 76.1 us (0.979)
  Pallas kernels: 71.8 us -> 74.7 us
  local copies, waits for them, and re-layouts: 2.84 us -> 0.02 us
  matrix products: 1.41 us -> 0 us
    pallas_call x0 -> x1, Pallas kernels: none -> 5.69 us  [finish(): pl.pallas_call(finish_kernel, grid=(D // tile,), out_shape=(jax.ShapeDtyp...]
    pallas_call x1, Pallas kernels: 71.8 us -> 69 us  [exchange(): pl.pallas_call(functools.partial(exchange_kernel, X, Z, J, slots, cell),...]
    unnamed x14 -> x8, local copies, waits for them, and re-layouts: 2.23 us -> 0.02 us
    dot_general x1 -> x0, matrix products: 1.41 us -> none  [dot(): lax.dot_general(a, b, (((ca,), (cb,)), ((), ())), preferred_element_type=...]
where the time goes in v3:
time: 76.1 us; the launch traced here: 76 us
  Pallas kernels  74.7 us (98%)
  between operations  1.26 us (2%)
    pallas_call x1, Pallas kernels, exchange(): pl.pallas_call(functools.partial(exchange_kernel, X, Z, J, slots, cell),...  69 us
    pallas_call x1, Pallas kernels, finish(): pl.pallas_call(finish_kernel, grid=(D // tile,), out_shape=(jax.ShapeDtyp...  5.69 us

profile of v3, /device:TPU:1, one launch (start us, length us, event | category | flops | bytes accessed | tf_op | source)
XLA Modules:
  0.0 76.0 jit_solution(13966600144483384476)
XLA Ops:
  0.6 0.0 copy-start.4
  0.6 0.0 copy-start.7
  0.7 0.0 copy-start.6
  0.7 0.0 copy-start.5
  0.7 69.0 %exchange_40_64.1 = (bf16[72,256]{1,0:T(8,128)(2,1)S(1)}, bf16[40,4608]{1,0:T(8,128)(2,1)S(1)}, bf16[40,512]{1,0:T(8,128)(2,1)S(1)}, bf16[256,256]{1,0:T(8,128)(2,1)S(1)}, s32[1,1]{1,0:T(1,128)}) custom-call(s32[4,256]{1,0:T(4,128)} %bitcast.7, bf16[256,256]{1,0:T(8,128)(2,1)} %codes_hbm.1, bf16[72,256]{1,0:T(8,128)(2,1)} %bitcast.5, f32[1,72]{1,0:T(1,128)} %bitcast.9, ...), custom_call_target="tpu_custom_call" | custom-call | tf_op jit(solution)/shard_map/exchange_40_64/pallas_call | solution.py:383
  70.2 0.0 copy-done.4
  70.2 0.0 copy-done.7
  70.3 0.0 copy-done.6
  70.3 0.0 copy-done.5
  70.3 5.7 %conditional.1 = ((bf16[72,256]{1,0:T(8,128)(2,1)}, bf16[512,4608]{1,0:T(8,128)(2,1)}, bf16[256,256]{1,0:T(8,128)(2,1)})) conditional(s32[]{:T(128)} %bitcast.3, (bf16[72,256]{1,0:T(8,128)(2,1)S(1)}, bf16[40,4608]{1,0:T(8,128)(2,1)S(1)}, bf16[40,512]{1,0:T(8,128)(2,1)S(1)}, bf16[256,256]{1,0:T(8,128)(2,1)S(1)}) %tuple.14, (s32[4,256]{1,0:T(4,128)S(1)}, ...), branch_computations={%region_0.0_spmd, %region_1.0_spmd} | conditional | flops 301989888 | bytes 8011896 | solution.py:493
  70.3 5.7 %finish_40.1 = (bf16[72,256]{1,0:T(8,128)(2,1)}, bf16[512,4608]{1,0:T(8,128)(2,1)}, bf16[256,256]{1,0:T(8,128)(2,1)}) custom-call(bf16[72,256]{1,0:T(8,128)(2,1)S(1)} %get-tuple-element.18.recon_in, bf16[40,4608]{1,0:T(8,128)(2,1)S(1)} %get-tuple-element.19.rows_ref, bf16[40,512]{1,0:T(8,128)(2,1)S(1)} %get-tuple-element.20.own_ref, ...), custom_call_target="tpu_custom_call" | custom-call | flops 188743680 | bytes 4718592 | tf_op jit(solution)/shard_map/cond/branch_0_fun/finish_40/pallas_call | solution.py:456
Async XLA Ops:
  0.6 69.6 %copy-start.4 = (bf16[256,256]{1,0:T(8,128)(2,1)S(1)}, bf16[256,256]{1,0:T(8,128)(2,1)}, u32[]{:S(2)}) copy-start(bf16[256,256]{1,0:T(8,128)(2,1)} %codes_hbm.1) | copy-start | bytes 393220
  0.6 69.6 %copy-start.7 = (f32[72]{0:T(128)S(1)}, f32[72]{0:T(128)}, u32[]{:S(2)}) copy-start(f32[72]{0:T(128)} %param.11) | copy-start | bytes 868
  0.7 69.6 %copy-start.6 = (s32[256,4]{0,1:T(4,128)S(1)}, s32[256,4]{0,1:T(4,128)}, u32[]{:S(2)}) copy-start(s32[256,4]{0,1:T(4,128)} %param.9) | copy-start | bytes 12292
  0.7 69.6 %copy-start.5 = (bf16[256,72]{0,1:T(8,128)(2,1)S(1)}, bf16[256,72]{0,1:T(8,128)(2,1)}, u32[]{:S(2)}) copy-start(bf16[256,72]{0,1:T(8,128)(2,1)} %param.7) | copy-start | bytes 110596

commit v4 on v3

--- a/solution.py
+++ b/solution.py
@@ -436,48 +436,51 @@
     )(ab, codes, act, bias, decoder)
 
 
-def finish_kernel(recon_in, rows_ref, own_ref, grad_in, recon_out, dgrad_ref, grad_out):
-    @pl.when(pl.program_id(0) == 0)
-    def _():
-        recon_out[...] = recon_in[...]
-        grad_out[...] = grad_in[...].T
-
-    dgrad_ref[...] = dot(own_ref[...], rows_ref[...], 0, 0).astype(BF16)
+def finish_kernel(
+    recon_in, rows, own, grad_in, recon_out, dgrad_out, grad_out, dgrad, grad, sem
+):
+    copies = [pltpu.make_async_copy(recon_in, recon_out, sem.at[0])]
+    copies[0].start()
+    parts = sem.shape[0] - 2
+    height = LATS // parts
+    for n in range(parts):
+        at = slice(n * height, (n + 1) * height)
+        dgrad[at, :] = dot(own[:, at], rows[...], 0, 0).astype(BF16)
+        copies.append(pltpu.make_async_copy(dgrad.at[at], dgrad_out.at[at], sem.at[2 + n]))
+        copies[-1].start()
+        if n == 0:
+            grad[...] = grad_in[...].T
+            copies.append(pltpu.make_async_copy(grad, grad_out, sem.at[1]))
+            copies[-1].start()
+    for copy in copies:
+        copy.wait()
 
 
 def finish(recon, rows, own, grad):
     slots, D = rows.shape
-    tile = 512 if D % 512 == 0 else D
     CO, T = grad.shape
-
-    def fixed(shape):
-        return pl.BlockSpec(shape, lambda n: (0, 0))
-
-    recon, decoder_grad, grad = pl.pallas_call(
+    whole = pl.BlockSpec(memory_space=pltpu.VMEM)
+    far = pl.BlockSpec(memory_space=pl.ANY)
+    return pl.pallas_call(
         finish_kernel,
-        grid=(D // tile,),
         out_shape=(
             jax.ShapeDtypeStruct(recon.shape, BF16),
             jax.ShapeDtypeStruct((LATS, D), BF16),
             jax.ShapeDtypeStruct((T, CO), BF16),
         ),
-        in_specs=[
-            fixed(recon.shape),
-            pl.BlockSpec((slots, tile), lambda n: (0, n)),
-            fixed(own.shape),
-            fixed(grad.shape),
+        in_specs=[whole] * 4,
+        out_specs=[far] * 3,
+        scratch_shapes=[
+            pltpu.VMEM((LATS, D), BF16),
+            pltpu.VMEM((T, CO), BF16),
+            pltpu.SemaphoreType.DMA((6,)),
         ],
-        out_specs=[
-            fixed(recon.shape),
-            pl.BlockSpec((LATS, tile), lambda n: (0, n)),
-            fixed((T, CO)),
-        ],
+        compiler_params=pltpu.CompilerParams(vmem_limit_bytes=32 * 2**20),
         cost_estimate=pl.CostEstimate(
             flops=2 * slots * LATS * D, bytes_accessed=2 * LATS * D, transcendentals=0
         ),
         name="finish_%d" % slots,
     )(recon, rows, own, grad)
-    return recon, decoder_grad, grad
 
 
 def per_device(J, activations, latent_codes, active_blocks, decoder, decoder_bias):

time: 76.1 us -> 73.6 us (0.967)
  Pallas kernels: 74.7 us -> 71.8 us
    pallas_call x1, Pallas kernels: 5.69 us -> 2.76 us  [finish(): pl.pallas_call(finish_kernel, out_shape=(jax.ShapeDtypeStruct(recon.shape...]
where the time goes in v4:
time: 73.6 us; the launch traced here: 73.5 us
  Pallas kernels  71.8 us (98%)
  between operations  1.49 us (2%)
    pallas_call x1, Pallas kernels, exchange(): pl.pallas_call(functools.partial(exchange_kernel, X, Z, J, slots, cell),...  69 us
    pallas_call x1, Pallas kernels, finish(): pl.pallas_call(finish_kernel, out_shape=(jax.ShapeDtypeStruct(recon.shape...  2.76 us

profile of v4, /device:TPU:1, one launch (start us, length us, event | category | flops | bytes accessed | tf_op | source)
XLA Modules:
  0.0 73.5 jit_solution(16882277594070832147)
XLA Ops:
  0.6 0.0 copy-start
  0.6 0.0 copy-start.3
  0.7 0.0 copy-start.2
  0.7 0.0 copy-start.1
  0.7 69.0 %exchange_40_64.1 = (bf16[72,256]{1,0:T(8,128)(2,1)S(1)}, bf16[40,4608]{1,0:T(8,128)(2,1)S(1)}, bf16[40,512]{1,0:T(8,128)(2,1)S(1)}, bf16[256,256]{1,0:T(8,128)(2,1)S(1)}, s32[1,1]{1,0:T(1,128)}) custom-call(s32[4,256]{1,0:T(4,128)} %bitcast.7, bf16[256,256]{1,0:T(8,128)(2,1)} %codes_hbm.1, bf16[72,256]{1,0:T(8,128)(2,1)} %bitcast.5, f32[1,72]{1,0:T(1,128)} %bitcast.9, ...), custom_call_target="tpu_custom_call" | custom-call | tf_op jit(solution)/shard_map/exchange_40_64/pallas_call | solution.py:383
  70.3 0.0 copy-done
  70.3 0.0 copy-done.3
  70.3 0.0 copy-done.2
  70.3 0.0 copy-done.1
  70.3 3.0 %conditional.1 = ((bf16[72,256]{1,0:T(8,128)(2,1)}, bf16[512,4608]{1,0:T(8,128)(2,1)}, bf16[256,256]{1,0:T(8,128)(2,1)})) conditional(s32[]{:T(128)} %bitcast.3, (bf16[72,256]{1,0:T(8,128)(2,1)S(1)}, bf16[40,4608]{1,0:T(8,128)(2,1)S(1)}, bf16[40,512]{1,0:T(8,128)(2,1)S(1)}, bf16[256,256]{1,0:T(8,128)(2,1)S(1)}) %tuple.14, (s32[4,256]{1,0:T(4,128)S(1)}, ...), branch_computations={%region_0.0_spmd, %region_1.0_spmd} | conditional | flops 301989888 | bytes 4718600 | solution.py:496
  70.3 2.8 %finish_40.1 = (bf16[72,256]{1,0:T(8,128)(2,1)}, bf16[512,4608]{1,0:T(8,128)(2,1)}, bf16[256,256]{1,0:T(8,128)(2,1)}) custom-call(bf16[72,256]{1,0:T(8,128)(2,1)S(1)} %get-tuple-element.18.recon_in, bf16[40,4608]{1,0:T(8,128)(2,1)S(1)} %get-tuple-element.19.rows, bf16[40,512]{1,0:T(8,128)(2,1)S(1)} %get-tuple-element.20.own, ...), custom_call_target="tpu_custom_call" | custom-call | flops 188743680 | bytes 4718592 | tf_op jit(solution)/shard_map/cond/branch_0_fun/finish_40/pallas_call | solution.py:464
Async XLA Ops:
  0.6 69.7 %copy-start = (bf16[256,256]{1,0:T(8,128)(2,1)S(1)}, bf16[256,256]{1,0:T(8,128)(2,1)}, u32[]{:S(2)}) copy-start(bf16[256,256]{1,0:T(8,128)(2,1)} %codes_hbm.1) | copy-start | bytes 393220
  0.6 69.7 %copy-start.3 = (f32[72]{0:T(128)S(1)}, f32[72]{0:T(128)}, u32[]{:S(2)}) copy-start(f32[72]{0:T(128)} %param.11) | copy-start | bytes 868
  0.7 69.7 %copy-start.2 = (s32[256,4]{0,1:T(4,128)S(1)}, s32[256,4]{0,1:T(4,128)}, u32[]{:S(2)}) copy-start(s32[256,4]{0,1:T(4,128)} %param.9) | copy-start | bytes 12292
  0.7 69.7 %copy-start.1 = (bf16[256,72]{0,1:T(8,128)(2,1)S(1)}, bf16[256,72]{0,1:T(8,128)(2,1)}, u32[]{:S(2)}) copy-start(bf16[256,72]{0,1:T(8,128)(2,1)} %param.7) | copy-start | bytes 110596

commit v5 on v4

--- a/solution.py
+++ b/solution.py
@@ -36,18 +36,19 @@
     return ones(iota((rows, place.shape[1]), 0) == place).astype(BF16)
 
 
-def onehot_twice(place, rows, pack):
-    ids = iota((rows * pack, place.shape[1]), 0)
+def twice_ids(rows, pack, width):
+    ids = iota((rows * pack, width), 0)
     if pack == 2:
         ids = jnp.where(ids >= rows, ids - rows, ids)
-    return ones(ids == place).astype(BF16)
-
-
-def member(key, ids):
-    named = key[0:1] == ids
-    for k in range(1, K_BLK):
-        named = named | (key[k : k + 1] == ids)
-    return ones(named)
+    return ids
+
+
+def onehot_twice(place, rows, pack):
+    return ones(twice_ids(rows, pack, place.shape[1]) == place).astype(BF16)
+
+
+def flat(key):
+    return jnp.concatenate([key[k : k + 1] for k in range(K_BLK)], axis=1)
 
 
 def exchange_kernel(
@@ -56,7 +57,7 @@
     recon_ref, rows, own, grad_ref, over_ref,
     ab_my, codes, act, bias, dec, ab_all, c_all, q_all, zt, places, codes_out, codes_in,
     part, a_out, a_in, gpt, b_out, b_in, packed, recon_bf, b2_out, b2_in,
-    a2_out, a2_in, yt, w_out, w_in, d_out, d_in, packed_d, g_in,
+    a2_out, a2_in, yt, w_out, w_in, d_out, d_in, packed_d, pc_all, grads, g_in,
     send_sem, recv_sem, in_sem,
 ):
     T = ab_my.shape[1]
@@ -66,7 +67,8 @@
     wide = cell * pack
     cw = act.shape[0]
     span = Z * cw
-    cs = CODES // J
+    cs = LAT_BLOCK // 2
+    PT = K_BLK * T
     D = dec.shape[1]
     top = b_out.shape[1]
     top_d = d_out.shape[1]
@@ -74,6 +76,7 @@
     lat = lax.axis_index("latent")
     z = lax.div(lat, J)
     j = lax.rem(lat, J)
+    core = lax.rem(j, 2)
     g = d * Z + z
 
     def to(me, n, r):
@@ -124,7 +127,7 @@
         return copy
 
     lanes = min(128, T)
-    per = T // lanes
+    per = PT // lanes
     upto = ones(iota((lanes, lanes), 0) <= iota((lanes, lanes), 1)).astype(BF16)
 
     def running(mem):
@@ -145,71 +148,70 @@
             named = mem[:, c * lanes : (c + 1) * lanes]
             pieces.append(jnp.where(named > 0.5, here - 1.0 + base, -1.0))
             base = base + here[:, lanes - 1 : lanes]
-        return jnp.concatenate(pieces, axis=1).astype(jnp.int32)
+        return jnp.concatenate(pieces, axis=1).astype(jnp.int32), base
 
     to_owner = int(math.log2(BLK_DEV))
     to_group = int(math.log2(J))
     for load in loads[:2]:
         load.wait()
     ab_here = ab_my[...]
-    owner_here = ab_here >> to_owner
-    mem = member(owner_here, (iota((X + (-X) % 8, 1), 0) * Z + z) * J + j)
-    along = placed(mem, running(mem), per)
+    flat_here = flat(ab_here)
+    owner_here = flat_here >> to_owner
+    mem = ones(owner_here == (iota((X + (-X) % 8, 1), 0) * Z + z) * J + j)
+    along, count = placed(mem, running(mem), per)
+    block = jnp.broadcast_to((flat_here & (BLK_DEV - 1)) + 1, (8, PT)).astype(F32).astype(BF16)
+    picks = [onehot(along[i : i + 1], slots) for i in range(X)]
     for i in range(X):
-        codes_out[i] = dot(onehot(along[i : i + 1], slots), codes[...]).astype(BF16)
+        pick = jnp.concatenate(
+            [picks[i][:, k * T : (k + 1) * T] for k in range(K_BLK)], axis=0
+        )
+        got = dot(pick, codes[...])
+        total = jnp.zeros((slots, LAT_BLOCK), F32)
+        for k in range(K_BLK):
+            total = total + got[
+                k * slots : (k + 1) * slots, k * LAT_BLOCK : (k + 1) * LAT_BLOCK
+            ]
+        codes_out[i] = jnp.concatenate(
+            [
+                total,
+                dot(picks[i], block, 1, 1),
+                jnp.broadcast_to(count[i : i + 1], (slots, 128 - LAT_BLOCK - 8)),
+            ],
+            axis=1,
+        ).astype(BF16)
     ab_all[d] = ab_here
     codes_in[d] = codes_out[d]
     pl.semaphore_wait(barrier, len(j_peers) + len(xz_peers))
 
     copies = []
     for r, peer in zip(x_steps, x_peers):
-        copies.append(put(ab_my, ab_all.at[d], peer))
         copies.append(put(codes_out.at[to(d, X, r)], codes_in.at[d], peer))
-
-    mem = member(owner_here >> to_group, iota((G, 1), 0))
-    places[...] = placed(mem, running(mem), per)
+    ab_copies = [put(ab_my, ab_all.at[d], peer) for peer in x_peers]
     loads[2].wait()
     loads[3].wait()
     column = jnp.broadcast_to(bias[...], (8, cw)).T[:, 0:1]
     offset = column - act[...].astype(F32)
-    for copy in copies:
-        copy.wait_recv()
-
-    ab = jnp.concatenate([ab_all[i] for i in range(X)], axis=1)
-    owner = ab >> to_owner
-    group = owner >> to_group
-    mem_j = member(owner, g * J + iota((J + (-J) % 8, 1), 0))
-    mem_own = member(owner, g * J + j + 0 * iota((8, 1), 0))
-    mem_group = member(group, g + 0 * iota((8, 1), 0))
-    n_j = mem_j.shape[0]
-    mem = jnp.concatenate([mem_j, mem_own, mem_group], axis=0)
-    run = running(mem)
-    in_owner = placed(mem, run, NT // lanes)
-    anew = placed(mem, run, per)
-    for i in range(J):
-        q_all[i] = onehot(in_owner[i : i + 1], slots)
-    own_q = q_all[j]
-    named = jnp.where(owner == g * J + j, (ab & (BLK_DEV - 1)) + 1, 0)
-    named = jnp.concatenate([named.astype(F32), jnp.zeros((8 - K_BLK, NT), F32)], axis=0)
-    named = named.astype(BF16)
-    by_row = dot(own_q, named, 1, 1)
-    by_col = dot(named, own_q, 1, 1)
-    mine = jnp.zeros((slots, CODES), F32)
+    mem = ones((owner_here >> to_group) == iota((G, 1), 0))
+    places[...] = placed(mem, running(mem), per)[0]
+    for copy in copies:
+        copy.wait_recv()
+
+    mine = jnp.zeros((slots, 128), F32)
+    first = jnp.zeros((slots, 1), F32)
+    apart = (iota((slots, slots), 0) - iota((slots, slots), 1)).astype(F32)
     for i in range(X):
-        at = slice(i * T, (i + 1) * T)
-        pick = onehot(anew[n_j : n_j + 1, at], slots)
-        mine = mine + dot(dot(own_q[:, at], pick, 1, 1).astype(BF16), codes_in[i])
+        here = codes_in[i]
+        mine = mine + dot(ones(apart == first).astype(BF16), here)
+        first = first + here[:, 127:128].astype(F32)
+    by_row = mine[:, LAT_BLOCK : LAT_BLOCK + 1]
+    one = mine[:, :LAT_BLOCK]
+    twice = jnp.concatenate([one, one], axis=1)
     half = iota((slots, 2 * LAT_BLOCK), 1) >= LAT_BLOCK
-    twice = []
-    for k in range(K_BLK):
-        one = mine[:, k * LAT_BLOCK : (k + 1) * LAT_BLOCK]
-        twice.append(jnp.concatenate([one, one], axis=1))
     for m in range(BLK_DEV // 2):
         target = jnp.where(half, 2.0 * m + 2.0, 2.0 * m + 1.0)
-        total = jnp.zeros((slots, 2 * LAT_BLOCK), F32)
-        for k in range(K_BLK):
-            total = total + jnp.where(by_row[:, k : k + 1] == target, twice[k], 0.0)
-        own[:, m * 2 * LAT_BLOCK : (m + 1) * 2 * LAT_BLOCK] = total.astype(BF16)
+        own[:, m * 2 * LAT_BLOCK : (m + 1) * 2 * LAT_BLOCK] = jnp.where(
+            by_row == target, twice, 0.0
+        ).astype(BF16)
 
     loads[4].wait()
     tile = 512 if D % 512 == 0 else D
@@ -226,28 +228,31 @@
     for r, peer in zip(j_steps, j_peers):
         copies.append(put(a_out.at[to(j, J, r)], a_in.at[j], peer))
     a_in[j] = a_out[j]
-
-    def fill_c(i, carry):
-        c_all[i] = onehot_twice(places[pl.ds(i, 1), :], cell, pack)
-        return carry
-
-    lax.fori_loop(0, G, fill_c, 0)
+    for copy in ab_copies:
+        copy.wait_recv()
+    ab = jnp.concatenate([flat(ab_all[i]) for i in range(X)], axis=1)
+    owner = ab >> to_owner
+    group = owner >> to_group
+    mem = jnp.concatenate(
+        [
+            ones(owner == g * J + iota((J + (-J) % 8, 1), 0)),
+            ones(group == g + 0 * iota((8, 1), 0)),
+        ],
+        axis=0,
+    )
+    run = running(mem)
+    in_owner = placed(mem, run, X * per)[0]
+    anew = placed(mem, run, per)[0]
+    for i in range(J):
+        q_all[i] = onehot(in_owner[i : i + 1], slots)
     for i in range(X):
-        at = slice(i * T, (i + 1) * T)
-        pick = onehot_twice(anew[n_j + 8 : n_j + 9, at], cell, pack)
+        at = slice(i * PT, (i + 1) * PT)
+        pick = onehot_twice(anew[J + (-J) % 8 : J + (-J) % 8 + 1, at], cell, pack)
         zt[:, i * wide : (i + 1) * wide] = dot(
-            q_all[...].reshape(J * slots, NT)[:, at], pick, 1, 1
+            q_all[:, :, at].reshape(J * slots, PT), pick, 1, 1
         ).astype(BF16)
-    over = jnp.zeros((1, 1), F32)
-    part_of = min(64, G * J)
-    for i in range(G * J // part_of):
-        count = jnp.sum(member(owner, i * part_of + iota((part_of, 1), 0)), axis=1, keepdims=True)
-        over = over + jnp.max(ones(count > slots), axis=0, keepdims=True)
-    count = member(group, iota((G, 1), 0))
-    for i in range(X):
-        here = jnp.sum(count[:, i * T : (i + 1) * T], axis=1, keepdims=True)
-        over = over + jnp.max(ones(here > cell), axis=0, keepdims=True)
-    over_ref[0, 0] = jnp.max(over).astype(jnp.int32)
+    named = jnp.broadcast_to((ab & (BLK_DEV - 1)) + 1, (8, X * PT)).astype(F32).astype(BF16)
+    by_col = dot(named, q_all[j], 1, 1)[0:1]
     for copy in copies:
         copy.wait_recv()
 
@@ -281,6 +286,28 @@
     for (a, b), peer in zip(xz_steps, xz_peers):
         copies.append(put(b_out.at[to(d, X, a) * Z + to(z, Z, b)], b_in.at[g], peer))
     b_in[g] = b_out[g]
+
+    def fill_c(i, carry):
+        place = places[pl.ds(i, 1), :]
+        ids = twice_ids(cell, pack, T)
+        hit = ids == place[:, 0:T]
+        for k in range(1, K_BLK):
+            hit = hit | (ids == place[:, k * T : (k + 1) * T])
+        c_all[i] = ones(hit).astype(BF16)
+        return carry
+
+    lax.fori_loop(0, G, fill_c, 0)
+    over = jnp.zeros((1, 1), F32)
+    part_of = min(64, G * J)
+    for i in range(G * J // part_of):
+        mem = ones(owner == i * part_of + iota((part_of, 1), 0))
+        here = jnp.sum(mem, axis=1, keepdims=True)
+        over = over + jnp.max(ones(here > slots), axis=0, keepdims=True)
+    for i in range(X):
+        mem = ones(group[:, i * PT : (i + 1) * PT] == iota((G, 1), 0))
+        here = jnp.sum(mem, axis=1, keepdims=True)
+        over = over + jnp.max(ones(here > cell), axis=0, keepdims=True)
+    over_ref[0, 0] = jnp.max(over).astype(jnp.int32)
     for copy in copies:
         copy.wait_recv()
     for i in range(G):
@@ -301,6 +328,13 @@
             if a2 == a:
                 copies.append(put(b2_out.at[x * Z + to(z, Z, b)], b2_in.at[g], peer))
     b2_in[g] = b2_out[g]
+    if pack == 2:
+
+        def fill_pc(i, carry):
+            pc_all[i] = onehot(places[pl.ds(i, 1), :], cell)
+            return carry
+
+        lax.fori_loop(0, G, fill_pc, 0)
     for copy in copies:
         copy.wait_recv()
     pieces = []
@@ -308,8 +342,8 @@
         pieces.append(
             jnp.concatenate([unpacks(b2_in[i * Z + n], cw) for i in range(X)], axis=1).astype(F32)
         )
-    flat = jnp.concatenate(pieces, axis=0).astype(BF16)
-    a2_out[...] = dot(zt[...], flat, 1, 1).astype(BF16).reshape(J, slots, span)
+    full = jnp.concatenate(pieces, axis=0).astype(BF16)
+    a2_out[...] = dot(zt[...], full, 1, 1).astype(BF16).reshape(J, slots, span)
     copies = []
     for r, peer in zip(j_steps, j_peers):
         copies.append(put(a2_out.at[to(j, J, r)], a2_in.at[j], peer))
@@ -326,19 +360,17 @@
         rows[:, m * width : (m + 1) * width] = jnp.concatenate(pieces, axis=1)
 
     yt[...] = dot(dec[...], rows[...], 1, 1)
-    for k in range(K_BLK):
-        total = jnp.zeros((LAT_BLOCK, slots), F32)
-        for b in range(BLK_DEV):
-            total = total + jnp.where(
-                by_col[k : k + 1, :] == b + 1.0, yt[b * LAT_BLOCK : (b + 1) * LAT_BLOCK, :], 0.0
-            )
-        total = total.astype(BF16)
-        for n in range(LAT_BLOCK // cs):
-            w_out[k * (LAT_BLOCK // cs) + n] = total[n * cs : (n + 1) * cs]
+    total = jnp.zeros((LAT_BLOCK, slots), F32)
+    for b in range(BLK_DEV):
+        total = total + jnp.where(
+            by_col == b + 1.0, yt[b * LAT_BLOCK : (b + 1) * LAT_BLOCK, :], 0.0
+        )
+    for n in range(2):
+        w_out[n] = total[n * cs : (n + 1) * cs].astype(BF16)
     copies = []
     for r, peer in zip(j_steps, j_peers):
-        copies.append(put(w_out.at[to(j, J, r)], w_in.at[j], peer))
-    w_in[j] = w_out[j]
+        copies.append(put(w_out.at[lax.rem(to(j, J, r), 2)], w_in.at[j], peer))
+    w_in[j] = w_out[core]
     for copy in copies:
         copy.wait_recv()
     merged = dot(w_in[0], zt[0:slots, :])
@@ -352,15 +384,32 @@
     d_in[g] = d_out[d]
     for copy in copies:
         copy.wait_recv()
-    for i in range(G):
-        packed_d[:, i * wide : (i + 1) * wide] = unpacks(d_in[i], cs)
-    g_in[j] = dot(packed_d[...], c_all[...].reshape(G * wide, T)).astype(BF16)
-    copies = []
-    for r, peer in zip(j_steps, j_peers):
-        copies.append(put(g_in.at[j], g_in.at[j], peer))
-    for copy in copies:
-        copy.wait_recv()
-    grad_ref[...] = g_in[...].reshape(CODES, T)
+    if pack == 2:
+        for i in range(0, G, 2):
+            here, after = d_in[i].astype(F32), d_in[i + 1].astype(F32)
+            packed_d[:, i * cell : (i + 2) * cell] = jnp.concatenate(
+                [
+                    jnp.where(left_row, here, pltpu.roll(after, cell, 1)),
+                    jnp.where(left_row, pltpu.roll(here, cell, 1), after),
+                ],
+                axis=0,
+            ).astype(BF16)
+        grads[...] = dot(packed_d[...], pc_all[...].reshape(G * cell, PT))
+    else:
+        grads[...] = jnp.zeros_like(grads)
+
+        def gather(i, carry):
+            grads[...] += dot(d_in[i], onehot(places[pl.ds(i, 1), :], cell))
+            return carry
+
+        lax.fori_loop(0, G, gather, 0)
+    for k in range(K_BLK):
+        g_in[core, k] = grads[:, k * T : (k + 1) * T].astype(BF16)
+    copy = put(g_in.at[core], g_in.at[core], (d, z * J + j + 1 - 2 * core))
+    copy.wait_recv()
+    for k in range(K_BLK):
+        for n in range(2):
+            grad_ref[(2 * k + n) * cs : (2 * k + n + 1) * cs, :] = g_in[n, k]
     for copy in sent:
         copy.wait_send()
 
@@ -371,12 +420,13 @@
     NT = X * T
     G = X * Z
     span = Z * cw
-    cs = CODES // J
+    cs = LAT_BLOCK // 2
+    PT = K_BLK * T
     pack = 128 // cell if cell < 128 else 1
     wide = cell * pack
     top = cw if pack == 1 else -(-cw // 16) * 8
     top_d = cs if pack == 1 else cs // 2
-    n_copies = 2 * (X - 1) + 3 * (G - 1) + 4 * (J - 1)
+    n_copies = 2 * (X - 1) + 3 * (G - 1) + 3 * (J - 1) + 1
     vmem = pltpu.VMEM
     whole = pl.BlockSpec(memory_space=pltpu.VMEM)
     far = pl.BlockSpec(memory_space=pl.ANY)
@@ -399,11 +449,11 @@
             vmem((LATS, D), BF16),
             vmem((X, K_BLK, T), jnp.int32),
             vmem((G, wide, T), BF16),
-            vmem((J, slots, NT), BF16),
+            vmem((J, slots, X * PT), BF16),
             vmem((J * slots, X * wide), BF16),
-            vmem((G, T), jnp.int32),
-            vmem((X, slots, CODES), BF16),
-            vmem((X, slots, CODES), BF16),
+            vmem((G, PT), jnp.int32),
+            vmem((X, slots, 128), BF16),
+            vmem((X, slots, 128), BF16),
             vmem((slots, D), BF16),
             vmem((J, slots, span), BF16),
             vmem((J, slots, span), BF16),
@@ -417,12 +467,14 @@
             vmem((J, slots, span), BF16),
             vmem((J, slots, span), BF16),
             vmem((LATS, slots), F32),
-            vmem((J, cs, slots), BF16),
+            vmem((2, cs, slots), BF16),
             vmem((J, cs, slots), BF16),
             vmem((X, top_d, wide), BF16),
             vmem((G, top_d, wide), BF16),
-            vmem((cs, G * wide), BF16),
-            vmem((J, cs, T), BF16),
+            vmem((cs, G * cell), BF16),
+            vmem((G if pack == 2 else 1, cell, PT), BF16),
+            vmem((cs, PT), F32),
+            vmem((2, K_BLK, cs, T), BF16),
             pltpu.SemaphoreType.DMA((n_copies,)),
             pltpu.SemaphoreType.DMA((n_copies,)),
             pltpu.SemaphoreType.DMA((5,)),
@@ -491,7 +543,7 @@
     *fast, over = exchange(X, Z, J, 40, 64, 0, *args)
 
     def roomy():
-        return finish(*exchange(X, Z, J, MOST_DEV, T, 1, *args)[:4])
+        return finish(*exchange(X, Z, J, MOST_DEV, J * MOST_DEV, 1, *args)[:4])
 
     recon, decoder_grad, grad = lax.cond(over[0, 0] > 0, roomy, lambda: finish(*fast))
     return recon.T, decoder_grad, grad

time: 73.6 us -> 71.1 us (0.966)
  Pallas kernels: 71.8 us -> 69.2 us
    pallas_call x1, Pallas kernels: 69 us -> 66.4 us  [exchange(): pl.pallas_call(functools.partial(exchange_kernel, X, Z, J, slots, cell),...]
where the time goes in v5:
time: 71.1 us; the launch traced here: 71 us
  Pallas kernels  69.2 us (97%)
  between operations  1.51 us (2%)
    pallas_call x1, Pallas kernels, exchange(): pl.pallas_call(functools.partial(exchange_kernel, X, Z, J, slots, cell),...  66.4 us
    pallas_call x1, Pallas kernels, finish(): pl.pallas_call(finish_kernel, out_shape=(jax.ShapeDtypeStruct(recon.shape...  2.76 us

profile of v5, /device:TPU:1, one launch (start us, length us, event | category | flops | bytes accessed | tf_op | source)
XLA Modules:
  0.0 71.0 jit_solution(514306407177593362)
XLA Ops:
  0.6 0.0 copy-start
  0.6 0.0 copy-start.3
  0.7 0.0 copy-start.2
  0.7 0.0 copy-start.1
  0.7 66.4 %exchange_40_64.1 = (bf16[72,256]{1,0:T(8,128)(2,1)S(1)}, bf16[40,4608]{1,0:T(8,128)(2,1)S(1)}, bf16[40,512]{1,0:T(8,128)(2,1)S(1)}, bf16[256,256]{1,0:T(8,128)(2,1)S(1)}, s32[1,1]{1,0:T(1,128)}) custom-call(s32[4,256]{1,0:T(4,128)} %bitcast.7, bf16[256,256]{1,0:T(8,128)(2,1)} %codes_hbm.1, bf16[72,256]{1,0:T(8,128)(2,1)} %bitcast.5, f32[1,72]{1,0:T(1,128)} %bitcast.9, ...), custom_call_target="tpu_custom_call" | custom-call | tf_op jit(solution)/shard_map/exchange_40_64/pallas_call | solution.py:433
  67.8 0.0 copy-done
  67.8 0.0 copy-done.3
  67.8 0.0 copy-done.2
  67.8 0.0 copy-done.1
  67.8 3.0 %conditional.1 = ((bf16[72,256]{1,0:T(8,128)(2,1)}, bf16[512,4608]{1,0:T(8,128)(2,1)}, bf16[256,256]{1,0:T(8,128)(2,1)})) conditional(s32[]{:T(128)} %bitcast.3, (bf16[72,256]{1,0:T(8,128)(2,1)S(1)}, bf16[40,4608]{1,0:T(8,128)(2,1)S(1)}, bf16[40,512]{1,0:T(8,128)(2,1)S(1)}, bf16[256,256]{1,0:T(8,128)(2,1)S(1)}) %tuple.14, (s32[4,256]{1,0:T(4,128)S(1)}, ...), branch_computations={%region_0.0_spmd, %region_1.0_spmd} | conditional | flops 301989888 | bytes 4718600 | solution.py:548
  67.8 2.8 %finish_40.1 = (bf16[72,256]{1,0:T(8,128)(2,1)}, bf16[512,4608]{1,0:T(8,128)(2,1)}, bf16[256,256]{1,0:T(8,128)(2,1)}) custom-call(bf16[72,256]{1,0:T(8,128)(2,1)S(1)} %get-tuple-element.18.recon_in, bf16[40,4608]{1,0:T(8,128)(2,1)S(1)} %get-tuple-element.19.rows, bf16[40,512]{1,0:T(8,128)(2,1)S(1)} %get-tuple-element.20.own, ...), custom_call_target="tpu_custom_call" | custom-call | flops 188743680 | bytes 4718592 | tf_op jit(solution)/shard_map/cond/branch_0_fun/finish_40/pallas_call | solution.py:516
Async XLA Ops:
  0.6 67.1 %copy-start = (bf16[256,256]{1,0:T(8,128)(2,1)S(1)}, bf16[256,256]{1,0:T(8,128)(2,1)}, u32[]{:S(2)}) copy-start(bf16[256,256]{1,0:T(8,128)(2,1)} %codes_hbm.1) | copy-start | bytes 393220
  0.6 67.1 %copy-start.3 = (f32[72]{0:T(128)S(1)}, f32[72]{0:T(128)}, u32[]{:S(2)}) copy-start(f32[72]{0:T(128)} %param.11) | copy-start | bytes 868
  0.7 67.1 %copy-start.2 = (s32[256,4]{0,1:T(4,128)S(1)}, s32[256,4]{0,1:T(4,128)}, u32[]{:S(2)}) copy-start(s32[256,4]{0,1:T(4,128)} %param.9) | copy-start | bytes 12292
  0.7 67.1 %copy-start.1 = (bf16[256,72]{0,1:T(8,128)(2,1)S(1)}, bf16[256,72]{0,1:T(8,128)(2,1)}, u32[]{:S(2)}) copy-start(bf16[256,72]{0,1:T(8,128)(2,1)} %param.7) | copy-start | bytes 110596

commit v6 on v5

--- a/solution.py
+++ b/solution.py
@@ -56,8 +56,8 @@
     ab_hbm, codes_hbm, act_hbm, bias_hbm, dec_hbm,
     recon_ref, rows, own, grad_ref, over_ref,
     ab_my, codes, act, bias, dec, ab_all, c_all, q_all, zt, places, codes_out, codes_in,
-    part, a_out, a_in, gpt, b_out, b_in, packed, recon_bf, b2_out, b2_in,
-    a2_out, a2_in, yt, w_out, w_in, d_out, d_in, packed_d, pc_all, grads, g_in,
+    part, a_out, a_in, gpt, b_out, b_in, recon_bf, b2_out, b2_in,
+    a2_out, a2_in, dec_by, yt, w_out, w_in, d_out, d_in, pc_all, grads, g_in,
     send_sem, recv_sem, in_sem,
 ):
     T = ab_my.shape[1]
@@ -130,25 +130,32 @@
     per = PT // lanes
     upto = ones(iota((lanes, lanes), 0) <= iota((lanes, lanes), 1)).astype(BF16)
 
+    every = jnp.ones((lanes, lanes), BF16)
+
+    def before(n, chunks, restart):
+        shape = (n * chunks, n * chunks)
+        here, there = iota(shape, 0), iota(shape, 1)
+        same = (here & (n - 1)) == (there & (n - 1))
+        step = int(math.log2(n))
+        here, there = here >> step, there >> step
+        rest = int(math.log2(restart))
+        same = same & (there < here) & ((there >> rest) == (here >> rest))
+        return ones(same).astype(BF16)
+
     def running(mem):
         n = mem.shape[0]
         chunks = mem.shape[1] // lanes
         stacked = jnp.concatenate(
             [mem[:, c * lanes : (c + 1) * lanes] for c in range(chunks)], axis=0
         )
-        run = dot(stacked.astype(BF16), upto)
-        return [run[c * n : (c + 1) * n] for c in range(chunks)]
-
-    def placed(mem, run, restart):
-        pieces = []
-        base = jnp.zeros((mem.shape[0], 1), F32)
-        for c, here in enumerate(run):
-            if c % restart == 0:
-                base = jnp.zeros_like(base)
-            named = mem[:, c * lanes : (c + 1) * lanes]
-            pieces.append(jnp.where(named > 0.5, here - 1.0 + base, -1.0))
-            base = base + here[:, lanes - 1 : lanes]
-        return jnp.concatenate(pieces, axis=1).astype(jnp.int32), base
+        low = stacked.astype(BF16)
+        return n, chunks, stacked, dot(low, upto), dot(low, every).astype(BF16)
+
+    def placed(runs, prior):
+        n, chunks, stacked, run, totals = runs
+        place = jnp.where(stacked > 0.5, run - 1.0 + dot(prior, totals), -1.0)
+        place = place.astype(jnp.int32)
+        return jnp.concatenate([place[c * n : (c + 1) * n] for c in range(chunks)], axis=1)
 
     to_owner = int(math.log2(BLK_DEV))
     to_group = int(math.log2(J))
@@ -158,7 +165,8 @@
     flat_here = flat(ab_here)
     owner_here = flat_here >> to_owner
     mem = ones(owner_here == (iota((X + (-X) % 8, 1), 0) * Z + z) * J + j)
-    along, count = placed(mem, running(mem), per)
+    along = placed(running(mem), before(mem.shape[0], per, per))
+    count = jnp.sum(mem, axis=1, keepdims=True)
     block = jnp.broadcast_to((flat_here & (BLK_DEV - 1)) + 1, (8, PT)).astype(F32).astype(BF16)
     picks = [onehot(along[i : i + 1], slots) for i in range(X)]
     for i in range(X):
@@ -192,7 +200,7 @@
     column = jnp.broadcast_to(bias[...], (8, cw)).T[:, 0:1]
     offset = column - act[...].astype(F32)
     mem = ones((owner_here >> to_group) == iota((G, 1), 0))
-    places[...] = placed(mem, running(mem), per)[0]
+    places[...] = placed(running(mem), before(G, per, per))
     for copy in copies:
         copy.wait_recv()
 
@@ -241,8 +249,8 @@
         axis=0,
     )
     run = running(mem)
-    in_owner = placed(mem, run, X * per)[0]
-    anew = placed(mem, run, per)[0]
+    in_owner = placed(run, before(mem.shape[0], X * per, X * per))
+    anew = placed(run, before(mem.shape[0], X * per, per))
     for i in range(J):
         q_all[i] = onehot(in_owner[i : i + 1], slots)
     for i in range(X):
@@ -308,12 +316,19 @@
         here = jnp.sum(mem, axis=1, keepdims=True)
         over = over + jnp.max(ones(here > cell), axis=0, keepdims=True)
     over_ref[0, 0] = jnp.max(over).astype(jnp.int32)
-    for copy in copies:
-        copy.wait_recv()
-    for i in range(G):
-        packed[:, i * wide : (i + 1) * wide] = unpacks(b_in[i], cw)
-    flat_c = c_all[...].reshape(G * wide, T)
-    recon = (dot(packed[...], flat_c) + offset).astype(BF16)
+
+    def by_x(copies):
+        for a in sorted(range(X), key=lambda r: near(X, r)):
+            for (a2, b), copy in zip(xz_steps, copies):
+                if a2 == (X - a) % X:
+                    copy.wait_recv()
+            yield to(d, X, a) * Z
+
+    total = offset
+    for first in by_x(copies):
+        packed = jnp.concatenate([unpacks(b_in[first + n], cw) for n in range(Z)], axis=1)
+        total = total + dot(packed, c_all[pl.ds(first, Z)].reshape(Z * wide, T))
+    recon = total.astype(BF16)
     recon_ref[...] = recon
     recon_bf[...] = recon
 
@@ -335,6 +350,16 @@
             return carry
 
         lax.fori_loop(0, G, fill_pc, 0)
+
+    def order(n, carry):
+        at = pl.ds(pl.multiple_of(n * LAT_BLOCK, LAT_BLOCK), LAT_BLOCK)
+        for i in range(J):
+            dec_by[i, at, :] = jnp.concatenate(
+                [dec[at, (m * J + i) * cw : (m * J + i + 1) * cw] for m in range(Z)], axis=1
+            )
+        return carry
+
+    lax.fori_loop(0, LATS // LAT_BLOCK, order, 0)
     for copy in copies:
         copy.wait_recv()
     pieces = []
@@ -348,8 +373,22 @@
     for r, peer in zip(j_steps, j_peers):
         copies.append(put(a2_out.at[to(j, J, r)], a2_in.at[j], peer))
     a2_in[j] = a2_out[j]
-    for copy in copies:
+    yt[...] = dot(dec_by[j], a2_out[j], 1, 1)
+    for r, copy in reversed(list(zip(j_steps, copies))):
         copy.wait_recv()
+        i = frm(j, J, r)
+        yt[...] += dot(dec_by[i], a2_in[i], 1, 1)
+    total = jnp.zeros((LAT_BLOCK, slots), F32)
+    for b in range(BLK_DEV):
+        total = total + jnp.where(
+            by_col == b + 1.0, yt[b * LAT_BLOCK : (b + 1) * LAT_BLOCK, :], 0.0
+        )
+    for n in range(2):
+        w_out[n] = total[n * cs : (n + 1) * cs].astype(BF16)
+    copies = []
+    for r, peer in zip(j_steps, j_peers):
+        copies.append(put(w_out.at[lax.rem(to(j, J, r), 2)], w_in.at[j], peer))
+    w_in[j] = w_out[core]
     for m in range(Z // 2):
         pieces = [
             a2_in[i, :, n * cw : (n + 1) * cw]
@@ -358,19 +397,6 @@
         ]
         width = 2 * J * cw
         rows[:, m * width : (m + 1) * width] = jnp.concatenate(pieces, axis=1)
-
-    yt[...] = dot(dec[...], rows[...], 1, 1)
-    total = jnp.zeros((LAT_BLOCK, slots), F32)
-    for b in range(BLK_DEV):
-        total = total + jnp.where(
-            by_col == b + 1.0, yt[b * LAT_BLOCK : (b + 1) * LAT_BLOCK, :], 0.0
-        )
-    for n in range(2):
-        w_out[n] = total[n * cs : (n + 1) * cs].astype(BF16)
-    copies = []
-    for r, peer in zip(j_steps, j_peers):
-        copies.append(put(w_out.at[lax.rem(to(j, J, r), 2)], w_in.at[j], peer))
-    w_in[j] = w_out[core]
     for copy in copies:
         copy.wait_recv()
     merged = dot(w_in[0], zt[0:slots, :])
@@ -382,20 +408,27 @@
     for (a, b), peer in zip(xz_steps, xz_peers):
         copies.append(put(d_out.at[to(d, X, a)], d_in.at[g], peer))
     d_in[g] = d_out[d]
-    for copy in copies:
-        copy.wait_recv()
     if pack == 2:
-        for i in range(0, G, 2):
-            here, after = d_in[i].astype(F32), d_in[i + 1].astype(F32)
-            packed_d[:, i * cell : (i + 2) * cell] = jnp.concatenate(
-                [
-                    jnp.where(left_row, here, pltpu.roll(after, cell, 1)),
-                    jnp.where(left_row, pltpu.roll(here, cell, 1), after),
-                ],
-                axis=0,
-            ).astype(BF16)
-        grads[...] = dot(packed_d[...], pc_all[...].reshape(G * cell, PT))
+        for at, first in enumerate(by_x(copies)):
+            pieces = []
+            for n in range(0, Z, 2):
+                here, after = d_in[first + n].astype(F32), d_in[first + n + 1].astype(F32)
+                pieces.append(
+                    jnp.concatenate(
+                        [
+                            jnp.where(left_row, here, pltpu.roll(after, cell, 1)),
+                            jnp.where(left_row, pltpu.roll(here, cell, 1), after),
+                        ],
+                        axis=0,
+                    ).astype(BF16)
+                )
+            more = dot(
+                jnp.concatenate(pieces, axis=1), pc_all[pl.ds(first, Z)].reshape(Z * cell, PT)
+            )
+            grads[...] = more if at == 0 else grads[...] + more
     else:
+        for copy in copies:
+            copy.wait_recv()
         grads[...] = jnp.zeros_like(grads)
 
         def gather(i, carry):
@@ -460,18 +493,17 @@
             vmem((span, X * wide), F32),
             vmem((G, top, wide), BF16),
             vmem((G, top, wide), BF16),
-            vmem((cw, G * wide), BF16),
             vmem((cw, T), BF16),
             vmem((G, top, wide), BF16),
             vmem((G, top, wide), BF16),
             vmem((J, slots, span), BF16),
             vmem((J, slots, span), BF16),
+            vmem((J, LATS, span), BF16),
             vmem((LATS, slots), F32),
             vmem((2, cs, slots), BF16),
             vmem((J, cs, slots), BF16),
             vmem((X, top_d, wide), BF16),
             vmem((G, top_d, wide), BF16),
-            vmem((cs, G * cell), BF16),
             vmem((G if pack == 2 else 1, cell, PT), BF16),
             vmem((cs, PT), F32),
             vmem((2, K_BLK, cs, T), BF16),
@@ -525,7 +557,7 @@
         scratch_shapes=[
             pltpu.VMEM((LATS, D), BF16),
             pltpu.VMEM((T, CO), BF16),
-            pltpu.SemaphoreType.DMA((6,)),
+            pltpu.SemaphoreType.DMA((10,)),
         ],
         compiler_params=pltpu.CompilerParams(vmem_limit_bytes=32 * 2**20),
         cost_estimate=pl.CostEstimate(

time: 71.1 us -> 69.3 us (0.975)
  Pallas kernels: 69.2 us -> 67.5 us
    pallas_call x1, Pallas kernels: 66.4 us -> 64.8 us  [exchange(): pl.pallas_call(functools.partial(exchange_kernel, X, Z, J, slots, cell),...]
where the time goes in v6:
time: 69.3 us
  Pallas kernels  67.5 us (97%)
  between operations  1.51 us (2%)
    pallas_call x1, Pallas kernels, exchange(): pl.pallas_call(functools.partial(exchange_kernel, X, Z, J, slots, cell),...  64.8 us
    pallas_call x1, Pallas kernels, finish(): pl.pallas_call(finish_kernel, out_shape=(jax.ShapeDtypeStruct(recon.shape...  2.65 us

profile of v6, /device:TPU:1, one launch (start us, length us, event | category | flops | bytes accessed | tf_op | source)
XLA Modules:
  0.0 69.3 jit_solution(4823785081083340473)
XLA Ops:
  0.6 0.0 copy-start
  0.6 0.0 copy-start.3
  0.7 0.0 copy-start.2
  0.7 0.0 copy-start.1
  0.7 64.8 %exchange_40_64.1 = (bf16[72,256]{1,0:T(8,128)(2,1)S(1)}, bf16[40,4608]{1,0:T(8,128)(2,1)S(1)}, bf16[40,512]{1,0:T(8,128)(2,1)S(1)}, bf16[256,256]{1,0:T(8,128)(2,1)S(1)}, s32[1,1]{1,0:T(1,128)}) custom-call(s32[4,256]{1,0:T(4,128)} %bitcast.7, bf16[256,256]{1,0:T(8,128)(2,1)} %codes_hbm.1, bf16[72,256]{1,0:T(8,128)(2,1)} %bitcast.5, f32[1,72]{1,0:T(1,128)} %bitcast.9, ...), custom_call_target="tpu_custom_call" | custom-call | tf_op jit(solution)/shard_map/exchange_40_64/pallas_call | solution.py:466
  66.2 0.0 copy-done
  66.2 0.0 copy-done.3
  66.2 0.0 copy-done.2
  66.2 0.0 copy-done.1
  66.2 2.9 %conditional.1 = ((bf16[72,256]{1,0:T(8,128)(2,1)}, bf16[512,4608]{1,0:T(8,128)(2,1)}, bf16[256,256]{1,0:T(8,128)(2,1)})) conditional(s32[]{:T(128)} %bitcast.3, (bf16[72,256]{1,0:T(8,128)(2,1)S(1)}, bf16[40,4608]{1,0:T(8,128)(2,1)S(1)}, bf16[40,512]{1,0:T(8,128)(2,1)S(1)}, bf16[256,256]{1,0:T(8,128)(2,1)S(1)}) %tuple.14, (s32[4,256]{1,0:T(4,128)S(1)}, ...), branch_computations={%region_0.0_spmd, %region_1.0_spmd} | conditional | flops 301989888 | bytes 4718600 | solution.py:580
  66.2 2.6 %finish_40.1 = (bf16[72,256]{1,0:T(8,128)(2,1)}, bf16[512,4608]{1,0:T(8,128)(2,1)}, bf16[256,256]{1,0:T(8,128)(2,1)}) custom-call(bf16[72,256]{1,0:T(8,128)(2,1)S(1)} %get-tuple-element.18.recon_in, bf16[40,4608]{1,0:T(8,128)(2,1)S(1)} %get-tuple-element.19.rows, bf16[40,512]{1,0:T(8,128)(2,1)S(1)} %get-tuple-element.20.own, ...), custom_call_target="tpu_custom_call" | custom-call | flops 188743680 | bytes 4718592 | tf_op jit(solution)/shard_map/cond/branch_0_fun/finish_40/pallas_call | solution.py:548
Async XLA Ops:
  0.6 65.5 %copy-start = (bf16[256,256]{1,0:T(8,128)(2,1)S(1)}, bf16[256,256]{1,0:T(8,128)(2,1)}, u32[]{:S(2)}) copy-start(bf16[256,256]{1,0:T(8,128)(2,1)} %codes_hbm.1) | copy-start | bytes 393220
  0.6 65.5 %copy-start.3 = (f32[72]{0:T(128)S(1)}, f32[72]{0:T(128)}, u32[]{:S(2)}) copy-start(f32[72]{0:T(128)} %param.11) | copy-start | bytes 868
  0.7 65.5 %copy-start.2 = (s32[256,4]{0,1:T(4,128)S(1)}, s32[256,4]{0,1:T(4,128)}, u32[]{:S(2)}) copy-start(s32[256,4]{0,1:T(4,128)} %param.9) | copy-start | bytes 12292
  0.7 65.5 %copy-start.1 = (bf16[256,72]{0,1:T(8,128)(2,1)S(1)}, bf16[256,72]{0,1:T(8,128)(2,1)}, u32[]{:S(2)}) copy-start(bf16[256,72]{0,1:T(8,128)(2,1)} %param.7) | copy-start | bytes 110596

commit v7 on v6

--- a/solution.py
+++ b/solution.py
@@ -110,11 +110,11 @@
     for peer in j_peers + xz_peers:
         pl.semaphore_signal(barrier, inc=1, device_id=peer, device_id_type=MESH)
 
+    taken = [0]
     sent = []
 
-    def put(src, dst, device):
-        at = len(sent)
-        copy = pltpu.make_async_remote_copy(
+    def copy_of(src, dst, device, at):
+        return pltpu.make_async_remote_copy(
             src_ref=src,
             dst_ref=dst,
             send_sem=send_sem.at[at],
@@ -122,9 +122,34 @@
             device_id=device,
             device_id_type=MESH,
         )
-        copy.start()
-        sent.append(copy)
-        return copy
+
+    def send(messages, like):
+        at = taken[0]
+        taken[0] += 1
+        for src, dst, device in messages:
+            copy_of(src, dst, device, at).start()
+        all_of = like.at[0 : len(messages)]
+        whole = copy_of(all_of, all_of, messages[0][2], at)
+        sent.append(whole)
+        return whole
+
+    def drain():
+        while sent:
+            sent.pop().wait_send()
+
+    def send_xz(message, like):
+        copies = {}
+        for a in sorted(range(X), key=lambda r: -near(X, r)):
+            copies[a] = send(
+                [message(a, b) + (peer,) for (a2, b), peer in zip(xz_steps, xz_peers) if a2 == a],
+                like,
+            )
+        return copies
+
+    def by_x(copies):
+        for a in sorted(range(X), key=lambda r: near(X, r)):
+            copies[(X - a) % X].wait_recv()
+            yield to(d, X, a) * Z
 
     lanes = min(128, T)
     per = PT // lanes
@@ -191,18 +216,21 @@
     codes_in[d] = codes_out[d]
     pl.semaphore_wait(barrier, len(j_peers) + len(xz_peers))
 
-    copies = []
-    for r, peer in zip(x_steps, x_peers):
-        copies.append(put(codes_out.at[to(d, X, r)], codes_in.at[d], peer))
-    ab_copies = [put(ab_my, ab_all.at[d], peer) for peer in x_peers]
+    copies = send(
+        [
+            (codes_out.at[to(d, X, r)], codes_in.at[d], peer)
+            for r, peer in zip(x_steps, x_peers)
+        ],
+        codes_in,
+    )
+    ab_copies = send([(ab_my, ab_all.at[d], peer) for peer in x_peers], ab_all)
     loads[2].wait()
     loads[3].wait()
     column = jnp.broadcast_to(bias[...], (8, cw)).T[:, 0:1]
     offset = column - act[...].astype(F32)
     mem = ones((owner_here >> to_group) == iota((G, 1), 0))
     places[...] = placed(running(mem), before(G, per, per))
-    for copy in copies:
-        copy.wait_recv()
+    copies.wait_recv()
 
     mine = jnp.zeros((slots, 128), F32)
     first = jnp.zeros((slots, 1), F32)
@@ -232,12 +260,11 @@
         a_out[i] = jnp.concatenate(
             [part[:, (n * J + i) * cw : (n * J + i + 1) * cw] for n in range(Z)], axis=1
         )
-    copies = []
-    for r, peer in zip(j_steps, j_peers):
-        copies.append(put(a_out.at[to(j, J, r)], a_in.at[j], peer))
+    copies = send(
+        [(a_out.at[to(j, J, r)], a_in.at[j], peer) for r, peer in zip(j_steps, j_peers)], a_in
+    )
     a_in[j] = a_out[j]
-    for copy in ab_copies:
-        copy.wait_recv()
+    ab_copies.wait_recv()
     ab = jnp.concatenate([flat(ab_all[i]) for i in range(X)], axis=1)
     owner = ab >> to_owner
     group = owner >> to_group
@@ -261,8 +288,7 @@
         ).astype(BF16)
     named = jnp.broadcast_to((ab & (BLK_DEV - 1)) + 1, (8, X * PT)).astype(F32).astype(BF16)
     by_col = dot(named, q_all[j], 1, 1)[0:1]
-    for copy in copies:
-        copy.wait_recv()
+    copies.wait_recv()
 
     left = lax.rem(iota((8, wide), 1), 128) < 64
     left_row = left[0:1]
@@ -290,9 +316,9 @@
             b_out[i * Z + n] = packs(
                 gpt[n * cw : (n + 1) * cw, i * wide : (i + 1) * wide], top
             ).astype(BF16)
-    copies = []
-    for (a, b), peer in zip(xz_steps, xz_peers):
-        copies.append(put(b_out.at[to(d, X, a) * Z + to(z, Z, b)], b_in.at[g], peer))
+    copies = send_xz(
+        lambda a, b: (b_out.at[to(d, X, a) * Z + to(z, Z, b)], b_in.at[g]), b_in
+    )
     b_in[g] = b_out[g]
 
     def fill_c(i, carry):
@@ -305,6 +331,16 @@
         return carry
 
     lax.fori_loop(0, G, fill_c, 0)
+
+    def order(n, carry):
+        at = pl.ds(pl.multiple_of(n * LAT_BLOCK, LAT_BLOCK), LAT_BLOCK)
+        for i in range(J):
+            dec_by[i, at, :] = jnp.concatenate(
+                [dec[at, (m * J + i) * cw : (m * J + i + 1) * cw] for m in range(Z)], axis=1
+            )
+        return carry
+
+    lax.fori_loop(0, LATS // LAT_BLOCK, order, 0)
     over = jnp.zeros((1, 1), F32)
     part_of = min(64, G * J)
     for i in range(G * J // part_of):
@@ -317,13 +353,7 @@
         over = over + jnp.max(ones(here > cell), axis=0, keepdims=True)
     over_ref[0, 0] = jnp.max(over).astype(jnp.int32)
 
-    def by_x(copies):
-        for a in sorted(range(X), key=lambda r: near(X, r)):
-            for (a2, b), copy in zip(xz_steps, copies):
-                if a2 == (X - a) % X:
-                    copy.wait_recv()
-            yield to(d, X, a) * Z
-
+    drain()
     total = offset
     for first in by_x(copies):
         packed = jnp.concatenate([unpacks(b_in[first + n], cw) for n in range(Z)], axis=1)
@@ -339,9 +369,16 @@
         sends = dot(recon_bf[...], back_c, 1, 1)
         for n in range(Z):
             b2_out[x * Z + n] = packs(sends[:, n * wide : (n + 1) * wide], top).astype(BF16)
-        for (a2, b), peer in zip(xz_steps, xz_peers):
-            if a2 == a:
-                copies.append(put(b2_out.at[x * Z + to(z, Z, b)], b2_in.at[g], peer))
+        copies.append(
+            send(
+                [
+                    (b2_out.at[x * Z + to(z, Z, b)], b2_in.at[g], peer)
+                    for (a2, b), peer in zip(xz_steps, xz_peers)
+                    if a2 == a
+                ],
+                b2_in,
+            )
+        )
     b2_in[g] = b2_out[g]
     if pack == 2:
 
@@ -350,16 +387,6 @@
             return carry
 
         lax.fori_loop(0, G, fill_pc, 0)
-
-    def order(n, carry):
-        at = pl.ds(pl.multiple_of(n * LAT_BLOCK, LAT_BLOCK), LAT_BLOCK)
-        for i in range(J):
-            dec_by[i, at, :] = jnp.concatenate(
-                [dec[at, (m * J + i) * cw : (m * J + i + 1) * cw] for m in range(Z)], axis=1
-            )
-        return carry
-
-    lax.fori_loop(0, LATS // LAT_BLOCK, order, 0)
     for copy in copies:
         copy.wait_recv()
     pieces = []
@@ -369,9 +396,10 @@
         )
     full = jnp.concatenate(pieces, axis=0).astype(BF16)
     a2_out[...] = dot(zt[...], full, 1, 1).astype(BF16).reshape(J, slots, span)
-    copies = []
-    for r, peer in zip(j_steps, j_peers):
-        copies.append(put(a2_out.at[to(j, J, r)], a2_in.at[j], peer))
+    copies = [
+        send([(a2_out.at[to(j, J, r)], a2_in.at[j], peer)], a2_in)
+        for r, peer in zip(j_steps, j_peers)
+    ]
     a2_in[j] = a2_out[j]
     yt[...] = dot(dec_by[j], a2_out[j], 1, 1)
     for r, copy in reversed(list(zip(j_steps, copies))):
@@ -385,9 +413,13 @@
         )
     for n in range(2):
         w_out[n] = total[n * cs : (n + 1) * cs].astype(BF16)
-    copies = []
-    for r, peer in zip(j_steps, j_peers):
-        copies.append(put(w_out.at[lax.rem(to(j, J, r), 2)], w_in.at[j], peer))
+    copies = send(
+        [
+            (w_out.at[lax.rem(to(j, J, r), 2)], w_in.at[j], peer)
+            for r, peer in zip(j_steps, j_peers)
+        ],
+        w_in,
+    )
     w_in[j] = w_out[core]
     for m in range(Z // 2):
         pieces = [
@@ -397,16 +429,14 @@
         ]
         width = 2 * J * cw
         rows[:, m * width : (m + 1) * width] = jnp.concatenate(pieces, axis=1)
-    for copy in copies:
-        copy.wait_recv()
+    copies.wait_recv()
     merged = dot(w_in[0], zt[0:slots, :])
     for i in range(1, J):
         merged = merged + dot(w_in[i], zt[i * slots : (i + 1) * slots, :])
     for i in range(X):
         d_out[i] = packs(merged[:, i * wide : (i + 1) * wide], top_d).astype(BF16)
-    copies = []
-    for (a, b), peer in zip(xz_steps, xz_peers):
-        copies.append(put(d_out.at[to(d, X, a)], d_in.at[g], peer))
+    copies = send_xz(lambda a, b: (d_out.at[to(d, X, a)], d_in.at[g]), d_in)
+    drain()
     d_in[g] = d_out[d]
     if pack == 2:
         for at, first in enumerate(by_x(copies)):
@@ -427,7 +457,7 @@
             )
             grads[...] = more if at == 0 else grads[...] + more
     else:
-        for copy in copies:
+        for copy in copies.values():
             copy.wait_recv()
         grads[...] = jnp.zeros_like(grads)
 
@@ -438,13 +468,12 @@
         lax.fori_loop(0, G, gather, 0)
     for k in range(K_BLK):
         g_in[core, k] = grads[:, k * T : (k + 1) * T].astype(BF16)
-    copy = put(g_in.at[core], g_in.at[core], (d, z * J + j + 1 - 2 * core))
+    copy = send([(g_in.at[core], g_in.at[core], (d, z * J + j + 1 - 2 * core))], g_in)
     copy.wait_recv()
     for k in range(K_BLK):
         for n in range(2):
             grad_ref[(2 * k + n) * cs : (2 * k + n + 1) * cs, :] = g_in[n, k]
-    for copy in sent:
-        copy.wait_send()
+    drain()
 
 
 def exchange(X, Z, J, slots, cell, collective_id, ab, codes, act, bias, decoder):
@@ -459,7 +488,7 @@
     wide = cell * pack
     top = cw if pack == 1 else -(-cw // 16) * 8
     top_d = cs if pack == 1 else cs // 2
-    n_copies = 2 * (X - 1) + 3 * (G - 1) + 3 * (J - 1) + 1
+    n_copies = 3 * X + (J - 1) + 5
     vmem = pltpu.VMEM
     whole = pl.BlockSpec(memory_space=pltpu.VMEM)
     far = pl.BlockSpec(memory_space=pl.ANY)

time: 69.3 us -> 67.3 us (0.971)
  Pallas kernels: 67.5 us -> 65.4 us
    pallas_call x1, Pallas kernels: 64.8 us -> 62.8 us  [exchange(): pl.pallas_call(functools.partial(exchange_kernel, X, Z, J, slots, cell),...]
where the time goes in v7:
time: 67.3 us; the launch traced here: 67.2 us
  Pallas kernels  65.4 us (97%)
  between operations  1.51 us (2%)
    pallas_call x1, Pallas kernels, exchange(): pl.pallas_call(functools.partial(exchange_kernel, X, Z, J, slots, cell),...  62.8 us
    pallas_call x1, Pallas kernels, finish(): pl.pallas_call(finish_kernel, out_shape=(jax.ShapeDtypeStruct(recon.shape...  2.65 us

profile of v7, /device:TPU:1, one launch (start us, length us, event | category | flops | bytes accessed | tf_op | source)
XLA Modules:
  0.0 67.2 jit_solution(9592821546699267627)
XLA Ops:
  0.6 0.0 copy-start
  0.6 0.0 copy-start.3
  0.7 0.0 copy-start.2
  0.7 0.0 copy-start.1
  0.7 62.8 %exchange_40_64.1 = (bf16[72,256]{1,0:T(8,128)(2,1)S(1)}, bf16[40,4608]{1,0:T(8,128)(2,1)S(1)}, bf16[40,512]{1,0:T(8,128)(2,1)S(1)}, bf16[256,256]{1,0:T(8,128)(2,1)S(1)}, s32[1,1]{1,0:T(1,128)}) custom-call(s32[4,256]{1,0:T(4,128)} %bitcast.7, bf16[256,256]{1,0:T(8,128)(2,1)} %codes_hbm.1, bf16[72,256]{1,0:T(8,128)(2,1)} %bitcast.5, f32[1,72]{1,0:T(1,128)} %bitcast.9, ...), custom_call_target="tpu_custom_call" | custom-call | tf_op jit(solution)/shard_map/exchange_40_64/pallas_call | solution.py:495
  64.1 0.0 copy-done
  64.1 0.0 copy-done.3
  64.1 0.0 copy-done.2
  64.1 0.0 copy-done.1
  64.1 2.9 %conditional.1 = ((bf16[72,256]{1,0:T(8,128)(2,1)}, bf16[512,4608]{1,0:T(8,128)(2,1)}, bf16[256,256]{1,0:T(8,128)(2,1)})) conditional(s32[]{:T(128)} %bitcast.3, (bf16[72,256]{1,0:T(8,128)(2,1)S(1)}, bf16[40,4608]{1,0:T(8,128)(2,1)S(1)}, bf16[40,512]{1,0:T(8,128)(2,1)S(1)}, bf16[256,256]{1,0:T(8,128)(2,1)S(1)}) %tuple.14, (s32[4,256]{1,0:T(4,128)S(1)}, ...), branch_computations={%region_0.0_spmd, %region_1.0_spmd} | conditional | flops 301989888 | bytes 4718600 | solution.py:609
  64.1 2.6 %finish_40.1 = (bf16[72,256]{1,0:T(8,128)(2,1)}, bf16[512,4608]{1,0:T(8,128)(2,1)}, bf16[256,256]{1,0:T(8,128)(2,1)}) custom-call(bf16[72,256]{1,0:T(8,128)(2,1)S(1)} %get-tuple-element.18.recon_in, bf16[40,4608]{1,0:T(8,128)(2,1)S(1)} %get-tuple-element.19.rows, bf16[40,512]{1,0:T(8,128)(2,1)S(1)} %get-tuple-element.20.own, ...), custom_call_target="tpu_custom_call" | custom-call | flops 188743680 | bytes 4718592 | tf_op jit(solution)/shard_map/cond/branch_0_fun/finish_40/pallas_call | solution.py:577
Async XLA Ops:
  0.6 63.4 %copy-start = (bf16[256,256]{1,0:T(8,128)(2,1)S(1)}, bf16[256,256]{1,0:T(8,128)(2,1)}, u32[]{:S(2)}) copy-start(bf16[256,256]{1,0:T(8,128)(2,1)} %codes_hbm.1) | copy-start | bytes 393220
  0.6 63.4 %copy-start.3 = (f32[72]{0:T(128)S(1)}, f32[72]{0:T(128)}, u32[]{:S(2)}) copy-start(f32[72]{0:T(128)} %param.11) | copy-start | bytes 868
  0.7 63.4 %copy-start.2 = (s32[256,4]{0,1:T(4,128)S(1)}, s32[256,4]{0,1:T(4,128)}, u32[]{:S(2)}) copy-start(s32[256,4]{0,1:T(4,128)} %param.9) | copy-start | bytes 12292
  0.7 63.4 %copy-start.1 = (bf16[256,72]{0,1:T(8,128)(2,1)S(1)}, bf16[256,72]{0,1:T(8,128)(2,1)}, u32[]{:S(2)}) copy-start(bf16[256,72]{0,1:T(8,128)(2,1)} %param.7) | copy-start | bytes 110596

commit v8 on v7

--- a/solution.py
+++ b/solution.py
@@ -56,8 +56,8 @@
     ab_hbm, codes_hbm, act_hbm, bias_hbm, dec_hbm,
     recon_ref, rows, own, grad_ref, over_ref,
     ab_my, codes, act, bias, dec, ab_all, c_all, q_all, zt, places, codes_out, codes_in,
-    part, a_out, a_in, gpt, b_out, b_in, recon_bf, b2_out, b2_in,
-    a2_out, a2_in, dec_by, yt, w_out, w_in, d_out, d_in, pc_all, grads, g_in,
+    part, a_out, a_in, gpt, b_out, b_in, recon_bf, ba_out, ba_in, bb_out, bb_in,
+    aa_out, aa_in, ab_out, ab_in, dec_a, dec_b, yt, w_out, w_in, d_out, d_in, pc_all, grads, g_in,
     send_sem, recv_sem, in_sem,
 ):
     T = ab_my.shape[1]
@@ -68,6 +68,8 @@
     cw = act.shape[0]
     span = Z * cw
     cs = LAT_BLOCK // 2
+    fa = -(-cw // 16) * 8
+    fb = cw - fa
     PT = K_BLK * T
     D = dec.shape[1]
     top = b_out.shape[1]
@@ -335,9 +337,9 @@
     def order(n, carry):
         at = pl.ds(pl.multiple_of(n * LAT_BLOCK, LAT_BLOCK), LAT_BLOCK)
         for i in range(J):
-            dec_by[i, at, :] = jnp.concatenate(
-                [dec[at, (m * J + i) * cw : (m * J + i + 1) * cw] for m in range(Z)], axis=1
-            )
+            starts = [(m * J + i) * cw for m in range(Z)]
+            dec_a[i, at, :] = jnp.concatenate([dec[at, f : f + fa] for f in starts], axis=1)
+            dec_b[i, at, :] = jnp.concatenate([dec[at, f + fa : f + cw] for f in starts], axis=1)
         return carry
 
     lax.fori_loop(0, LATS // LAT_BLOCK, order, 0)
@@ -362,24 +364,25 @@
     recon_ref[...] = recon
     recon_bf[...] = recon
 
-    copies = []
+    first_copies, later = [], []
     for a in sorted(range(X), key=lambda r: -near(X, r)):
         x = to(d, X, a)
         back_c = c_all[pl.ds(x * Z, Z)].reshape(Z * wide, T)
         sends = dot(recon_bf[...], back_c, 1, 1)
         for n in range(Z):
-            b2_out[x * Z + n] = packs(sends[:, n * wide : (n + 1) * wide], top).astype(BF16)
-        copies.append(
-            send(
-                [
-                    (b2_out.at[x * Z + to(z, Z, b)], b2_in.at[g], peer)
-                    for (a2, b), peer in zip(xz_steps, xz_peers)
-                    if a2 == a
-                ],
-                b2_in,
-            )
-        )
-    b2_in[g] = b2_out[g]
+            piece = sends[:, n * wide : (n + 1) * wide]
+            ba_out[x * Z + n] = packs(piece[:fa], ba_out.shape[1]).astype(BF16)
+            bb_out[x * Z + n] = packs(piece[fa:], bb_out.shape[1]).astype(BF16)
+        ways = [
+            (x * Z + to(z, Z, b), peer)
+            for (a2, b), peer in zip(xz_steps, xz_peers)
+            if a2 == a
+        ]
+        first_copies.append(send([(ba_out.at[i], ba_in.at[g], peer) for i, peer in ways], ba_in))
+        later.append([(bb_out.at[i], bb_in.at[g], peer) for i, peer in ways])
+    later_copies = [send(messages, bb_in) for messages in later]
+    ba_in[g] = ba_out[g]
+    bb_in[g] = bb_out[g]
     if pack == 2:
 
         def fill_pc(i, carry):
@@ -387,25 +390,36 @@
             return carry
 
         lax.fori_loop(0, G, fill_pc, 0)
-    for copy in copies:
-        copy.wait_recv()
-    pieces = []
-    for n in range(Z):
-        pieces.append(
-            jnp.concatenate([unpacks(b2_in[i * Z + n], cw) for i in range(X)], axis=1).astype(F32)
-        )
-    full = jnp.concatenate(pieces, axis=0).astype(BF16)
-    a2_out[...] = dot(zt[...], full, 1, 1).astype(BF16).reshape(J, slots, span)
-    copies = [
-        send([(a2_out.at[to(j, J, r)], a2_in.at[j], peer)], a2_in)
-        for r, peer in zip(j_steps, j_peers)
-    ]
-    a2_in[j] = a2_out[j]
-    yt[...] = dot(dec_by[j], a2_out[j], 1, 1)
-    for r, copy in reversed(list(zip(j_steps, copies))):
+
+    def returned(copies, src, rows):
+        for copy in copies:
+            copy.wait_recv()
+        pieces = [
+            jnp.concatenate([unpacks(src[i * Z + n], rows) for i in range(X)], axis=1).astype(F32)
+            for n in range(Z)
+        ]
+        return jnp.concatenate(pieces, axis=0).astype(BF16)
+
+    def to_owners(full, out, dst):
+        out[...] = dot(zt[...], full, 1, 1).astype(BF16).reshape(out.shape)
+        copies = [
+            send([(out.at[to(j, J, r)], dst.at[j], peer)], dst)
+            for r, peer in zip(j_steps, j_peers)
+        ]
+        dst[j] = out[j]
+        return copies
+
+    a_copies = to_owners(returned(first_copies, ba_in, fa), aa_out, aa_in)
+    b_copies = to_owners(returned(later_copies, bb_in, fb), ab_out, ab_in)
+    yt[...] = dot(dec_a[j], aa_out[j], 1, 1) + dot(dec_b[j], ab_out[j], 1, 1)
+    for r, copy in reversed(list(zip(j_steps, a_copies))):
         copy.wait_recv()
         i = frm(j, J, r)
-        yt[...] += dot(dec_by[i], a2_in[i], 1, 1)
+        yt[...] += dot(dec_a[i], aa_in[i], 1, 1)
+    for r, copy in reversed(list(zip(j_steps, b_copies))):
+        copy.wait_recv()
+        i = frm(j, J, r)
+        yt[...] += dot(dec_b[i], ab_in[i], 1, 1)
     total = jnp.zeros((LAT_BLOCK, slots), F32)
     for b in range(BLK_DEV):
         total = total + jnp.where(
@@ -423,9 +437,10 @@
     w_in[j] = w_out[core]
     for m in range(Z // 2):
         pieces = [
-            a2_in[i, :, n * cw : (n + 1) * cw]
+            half_in[i, :, n * rows_of : (n + 1) * rows_of]
             for n in (2 * m, 2 * m + 1)
             for i in range(J)
+            for half_in, rows_of in ((aa_in, fa), (ab_in, fb))
         ]
         width = 2 * J * cw
         rows[:, m * width : (m + 1) * width] = jnp.concatenate(pieces, axis=1)
@@ -483,12 +498,14 @@
     G = X * Z
     span = Z * cw
     cs = LAT_BLOCK // 2
+    fa = -(-cw // 16) * 8
+    fb = cw - fa
     PT = K_BLK * T
     pack = 128 // cell if cell < 128 else 1
     wide = cell * pack
     top = cw if pack == 1 else -(-cw // 16) * 8
     top_d = cs if pack == 1 else cs // 2
-    n_copies = 3 * X + (J - 1) + 5
+    n_copies = 4 * X + 2 * (J - 1) + 5
     vmem = pltpu.VMEM
     whole = pl.BlockSpec(memory_space=pltpu.VMEM)
     far = pl.BlockSpec(memory_space=pl.ANY)
@@ -523,11 +540,16 @@
             vmem((G, top, wide), BF16),
             vmem((G, top, wide), BF16),
             vmem((cw, T), BF16),
-            vmem((G, top, wide), BF16),
-            vmem((G, top, wide), BF16),
-            vmem((J, slots, span), BF16),
-            vmem((J, slots, span), BF16),
-            vmem((J, LATS, span), BF16),
+            vmem((G, fa // pack + (-(fa // pack)) % 8, wide), BF16),
+            vmem((G, fa // pack + (-(fa // pack)) % 8, wide), BF16),
+            vmem((G, fb // pack, wide), BF16),
+            vmem((G, fb // pack, wide), BF16),
+            vmem((J, slots, Z * fa), BF16),
+            vmem((J, slots, Z * fa), BF16),
+            vmem((J, slots, Z * fb), BF16),
+            vmem((J, slots, Z * fb), BF16),
+            vmem((J, LATS, Z * fa), BF16),
+            vmem((J, LATS, Z * fb), BF16),
             vmem((LATS, slots), F32),
             vmem((2, cs, slots), BF16),
             vmem((J, cs, slots), BF16),

time: 67.3 us -> 66.7 us (level)
  no operation moved by 1% of the time
where the time goes in v8:
time: 66.7 us
  Pallas kernels  65 us (97%)
  between operations  1.49 us (2%)
    pallas_call x1, Pallas kernels, exchange(): pl.pallas_call(functools.partial(exchange_kernel, X, Z, J, slots, cell),...  62.3 us
    pallas_call x1, Pallas kernels, finish(): pl.pallas_call(finish_kernel, out_shape=(jax.ShapeDtypeStruct(recon.shape...  2.65 us

profile of v8, /device:TPU:1, one launch (start us, length us, event | category | flops | bytes accessed | tf_op | source)
XLA Modules:
  0.0 66.7 jit_solution(17827745219650435184)
XLA Ops:
  0.6 0.0 copy-start
  0.6 0.0 copy-start.3
  0.7 0.0 copy-start.2
  0.7 0.0 copy-start.1
  0.7 62.3 %exchange_40_64.1 = (bf16[72,256]{1,0:T(8,128)(2,1)S(1)}, bf16[40,4608]{1,0:T(8,128)(2,1)S(1)}, bf16[40,512]{1,0:T(8,128)(2,1)S(1)}, bf16[256,256]{1,0:T(8,128)(2,1)S(1)}, s32[1,1]{1,0:T(1,128)}) custom-call(s32[4,256]{1,0:T(4,128)} %bitcast.7, bf16[256,256]{1,0:T(8,128)(2,1)} %codes_hbm.1, bf16[72,256]{1,0:T(8,128)(2,1)} %bitcast.5, f32[1,72]{1,0:T(1,128)} %bitcast.9, ...), custom_call_target="tpu_custom_call" | custom-call | tf_op jit(solution)/shard_map/exchange_40_64/pallas_call | solution.py:512
  63.6 0.0 copy-done
  63.6 0.0 copy-done.3
  63.6 0.0 copy-done.2
  63.6 0.0 copy-done.1
  63.6 2.8 %conditional.1 = ((bf16[72,256]{1,0:T(8,128)(2,1)}, bf16[512,4608]{1,0:T(8,128)(2,1)}, bf16[256,256]{1,0:T(8,128)(2,1)})) conditional(s32[]{:T(128)} %bitcast.3, (bf16[72,256]{1,0:T(8,128)(2,1)S(1)}, bf16[40,4608]{1,0:T(8,128)(2,1)S(1)}, bf16[40,512]{1,0:T(8,128)(2,1)S(1)}, bf16[256,256]{1,0:T(8,128)(2,1)S(1)}) %tuple.14, (s32[4,256]{1,0:T(4,128)S(1)}, ...), branch_computations={%region_0.0_spmd, %region_1.0_spmd} | conditional | flops 301989888 | bytes 4718600 | solution.py:631
  63.8 2.6 %finish_40.1 = (bf16[72,256]{1,0:T(8,128)(2,1)}, bf16[512,4608]{1,0:T(8,128)(2,1)}, bf16[256,256]{1,0:T(8,128)(2,1)}) custom-call(bf16[72,256]{1,0:T(8,128)(2,1)S(1)} %get-tuple-element.18.recon_in, bf16[40,4608]{1,0:T(8,128)(2,1)S(1)} %get-tuple-element.19.rows, bf16[40,512]{1,0:T(8,128)(2,1)S(1)} %get-tuple-element.20.own, ...), custom_call_target="tpu_custom_call" | custom-call | flops 188743680 | bytes 4718592 | tf_op jit(solution)/shard_map/cond/branch_0_fun/finish_40/pallas_call | solution.py:599
Async XLA Ops:
  0.6 63.0 %copy-start = (bf16[256,256]{1,0:T(8,128)(2,1)S(1)}, bf16[256,256]{1,0:T(8,128)(2,1)}, u32[]{:S(2)}) copy-start(bf16[256,256]{1,0:T(8,128)(2,1)} %codes_hbm.1) | copy-start | bytes 393220
  0.6 63.0 %copy-start.3 = (f32[72]{0:T(128)S(1)}, f32[72]{0:T(128)}, u32[]{:S(2)}) copy-start(f32[72]{0:T(128)} %param.11) | copy-start | bytes 868
  0.7 63.0 %copy-start.2 = (s32[256,4]{0,1:T(4,128)S(1)}, s32[256,4]{0,1:T(4,128)}, u32[]{:S(2)}) copy-start(s32[256,4]{0,1:T(4,128)} %param.9) | copy-start | bytes 12292
  0.7 63.0 %copy-start.1 = (bf16[256,72]{0,1:T(8,128)(2,1)S(1)}, bf16[256,72]{0,1:T(8,128)(2,1)}, u32[]{:S(2)}) copy-start(bf16[256,72]{0,1:T(8,128)(2,1)} %param.7) | copy-start | bytes 110596

commit v9 on v8

--- a/solution.py
+++ b/solution.py
@@ -400,20 +400,20 @@
         ]
         return jnp.concatenate(pieces, axis=0).astype(BF16)
 
-    def to_owners(full, out, dst):
+    def to_owners(full, out, dst, together):
         out[...] = dot(zt[...], full, 1, 1).astype(BF16).reshape(out.shape)
-        copies = [
-            send([(out.at[to(j, J, r)], dst.at[j], peer)], dst)
-            for r, peer in zip(j_steps, j_peers)
+        messages = [
+            (out.at[to(j, J, r)], dst.at[j], peer) for r, peer in zip(j_steps, j_peers)
         ]
+        copies = [send(messages, dst)] if together else [send([m], dst) for m in messages]
         dst[j] = out[j]
         return copies
 
-    a_copies = to_owners(returned(first_copies, ba_in, fa), aa_out, aa_in)
-    b_copies = to_owners(returned(later_copies, bb_in, fb), ab_out, ab_in)
+    a_copies = to_owners(returned(first_copies, ba_in, fa), aa_out, aa_in, True)
+    b_copies = to_owners(returned(later_copies, bb_in, fb), ab_out, ab_in, False)
     yt[...] = dot(dec_a[j], aa_out[j], 1, 1) + dot(dec_b[j], ab_out[j], 1, 1)
-    for r, copy in reversed(list(zip(j_steps, a_copies))):
-        copy.wait_recv()
+    a_copies[0].wait_recv()
+    for r in j_steps:
         i = frm(j, J, r)
         yt[...] += dot(dec_a[i], aa_in[i], 1, 1)
     for r, copy in reversed(list(zip(j_steps, b_copies))):

time: 66.7 us -> 66.3 us (level)
  no operation moved by 1% of the time
where the time goes in v9:
time: 66.3 us; the launch traced here: 66.2 us
  Pallas kernels  64.5 us (97%)
  between operations  1.49 us (2%)
    pallas_call x1, Pallas kernels, exchange(): pl.pallas_call(functools.partial(exchange_kernel, X, Z, J, slots, cell),...  61.8 us
    pallas_call x1, Pallas kernels, finish(): pl.pallas_call(finish_kernel, out_shape=(jax.ShapeDtypeStruct(recon.shape...  2.65 us

profile of v9, /device:TPU:1, one launch (start us, length us, event | category | flops | bytes accessed | tf_op | source)
XLA Modules:
  0.0 66.2 jit_solution(14980225584457989865)
XLA Ops:
  0.6 0.0 copy-start
  0.6 0.0 copy-start.3
  0.7 0.0 copy-start.2
  0.7 0.0 copy-start.1
  0.7 61.8 %exchange_40_64.1 = (bf16[72,256]{1,0:T(8,128)(2,1)S(1)}, bf16[40,4608]{1,0:T(8,128)(2,1)S(1)}, bf16[40,512]{1,0:T(8,128)(2,1)S(1)}, bf16[256,256]{1,0:T(8,128)(2,1)S(1)}, s32[1,1]{1,0:T(1,128)}) custom-call(s32[4,256]{1,0:T(4,128)} %bitcast.7, bf16[256,256]{1,0:T(8,128)(2,1)} %codes_hbm.1, bf16[72,256]{1,0:T(8,128)(2,1)} %bitcast.5, f32[1,72]{1,0:T(1,128)} %bitcast.9, ...), custom_call_target="tpu_custom_call" | custom-call | tf_op jit(solution)/shard_map/exchange_40_64/pallas_call | solution.py:512
  63.1 0.0 copy-done
  63.2 0.0 copy-done.3
  63.2 0.0 copy-done.2
  63.2 0.0 copy-done.1
  63.2 2.8 %conditional.1 = ((bf16[72,256]{1,0:T(8,128)(2,1)}, bf16[512,4608]{1,0:T(8,128)(2,1)}, bf16[256,256]{1,0:T(8,128)(2,1)})) conditional(s32[]{:T(128)} %bitcast.3, (bf16[72,256]{1,0:T(8,128)(2,1)S(1)}, bf16[40,4608]{1,0:T(8,128)(2,1)S(1)}, bf16[40,512]{1,0:T(8,128)(2,1)S(1)}, bf16[256,256]{1,0:T(8,128)(2,1)S(1)}) %tuple.14, (s32[4,256]{1,0:T(4,128)S(1)}, ...), branch_computations={%region_0.0_spmd, %region_1.0_spmd} | conditional | flops 301989888 | bytes 4718600 | solution.py:631
  63.4 2.6 %finish_40.1 = (bf16[72,256]{1,0:T(8,128)(2,1)}, bf16[512,4608]{1,0:T(8,128)(2,1)}, bf16[256,256]{1,0:T(8,128)(2,1)}) custom-call(bf16[72,256]{1,0:T(8,128)(2,1)S(1)} %get-tuple-element.18.recon_in, bf16[40,4608]{1,0:T(8,128)(2,1)S(1)} %get-tuple-element.19.rows, bf16[40,512]{1,0:T(8,128)(2,1)S(1)} %get-tuple-element.20.own, ...), custom_call_target="tpu_custom_call" | custom-call | flops 188743680 | bytes 4718592 | tf_op jit(solution)/shard_map/cond/branch_0_fun/finish_40/pallas_call | solution.py:599
Async XLA Ops:
  0.6 62.5 %copy-start = (bf16[256,256]{1,0:T(8,128)(2,1)S(1)}, bf16[256,256]{1,0:T(8,128)(2,1)}, u32[]{:S(2)}) copy-start(bf16[256,256]{1,0:T(8,128)(2,1)} %codes_hbm.1) | copy-start | bytes 393220
  0.6 62.5 %copy-start.3 = (f32[72]{0:T(128)S(1)}, f32[72]{0:T(128)}, u32[]{:S(2)}) copy-start(f32[72]{0:T(128)} %param.11) | copy-start | bytes 868
  0.7 62.5 %copy-start.2 = (s32[256,4]{0,1:T(4,128)S(1)}, s32[256,4]{0,1:T(4,128)}, u32[]{:S(2)}) copy-start(s32[256,4]{0,1:T(4,128)} %param.9) | copy-start | bytes 12292
  0.7 62.5 %copy-start.1 = (bf16[256,72]{0,1:T(8,128)(2,1)S(1)}, bf16[256,72]{0,1:T(8,128)(2,1)}, u32[]{:S(2)}) copy-start(bf16[256,72]{0,1:T(8,128)(2,1)} %param.7) | copy-start | bytes 110596
